TPU v7x, 32 devices: a whole 2x2x4 slice. The times are simulated.
32 devices in a mesh: lon: 8 (over z, x), lat: 4 (over y, core).
Axes of the slice: x: 2, y: 2, z: 4, core: 2. Of those that a mesh axis runs over, the one named last changes fastest.
Arguments:
- right_side: float32 [2, 32, 64, 1024], P(None, None, 'lat', 'lon'), may hold values from -36 to 36
- sea_mask: int32 [32, 64, 1024], P(None, 'lat', 'lon'), may hold values 0 or 1
- levels: int32 [64, 1024], P('lat', 'lon'), may hold values from 0 to 32
- east_diffusivity: bfloat16 [32, 64, 1024], P(None, 'lat', 'lon'), may hold values from 1 to 8
- north_diffusivity: bfloat16 [32, 64, 1024], P(None, 'lat', 'lon'), may hold values from 1 to 8
- vertical_diffusivity: bfloat16 [32, 64, 1024], P(None, 'lat', 'lon'), may hold values from 0.5 to 8
Outputs:
- solution_field: float32 [2, 32, 64, 1024], P(None, None, 'lat', 'lon')
- residual: float32 [2, 32, 64, 1024], P(None, None, 'lat', 'lon')
All inputs are finite; a program needn't handle non-finite values. No bound on the sum of `sea_mask` on one device may be relied on, other than what follows from the above.
Results may differ from a plain program's by a relative error of at most 0.004.
Values sent between devices are 32-bit elements; how exact they have to be, the bound alone decides.
No kernel may reach another device: no remote copies, remote signals or barrier semaphores. Data moves between devices by JAX's collectives and lax.ppermute only.
A program may use at most 64 MiB of HBM per device.

v0:
```python
import functools

import jax
import jax.numpy as jnp
from jax import lax
from jax.experimental import pallas as pl
from jax.experimental.pallas import tpu as pltpu
from jax.sharding import PartitionSpec as P

F32 = jnp.float32
CHUNK = 8
SHARES = 4
SIDES = 2
FIELDS = 5


def iota(shape, axis):
    return lax.broadcasted_iota(jnp.int32, shape, axis)


def is_even(axis):
    return (lax.axis_index(axis) & 1) == 0


def levels_of(ref, first, count, rows):
    return ref[pl.ds(first * rows, count * rows), :].reshape(count, rows, ref.shape[1])


def put_levels(ref, first, value):
    count, rows, lanes = value.shape
    ref[pl.ds(first * rows, count * rows), :] = value.reshape(count * rows, lanes)


def laplacian(value, below, flux_above, coefs):
    _, rows, lanes = value.shape
    east, west, north, south, down = coefs
    change = east * (value - pltpu.roll(value, lanes - 1, 2)) + west * (value - pltpu.roll(value, 1, 2))
    change = change + (north * (value - pltpu.roll(value, rows - 1, 1)) + south * (value - pltpu.roll(value, 1, 1)))
    flux_down = down * (jnp.concatenate([value[1:], below], axis=0) - value)
    from_above = jnp.concatenate([flux_above, flux_down[:-1]], axis=0)
    return change + (from_above - flux_down), flux_down[-1:]


def packed_into(total, planes, first, step, pair):
    slots = [first + step * i for i in range(planes.shape[0])]
    moved = [pltpu.roll(planes[i], 2 * slot + 1, 1) for i, slot in enumerate(slots)]
    for slot, plane in zip(slots, moved):
        total = jnp.where(pair == slot, plane, total)
    return total


def unpacked(packed, first, step, count, offset=1):
    lanes = packed.shape[1]
    return jnp.stack([pltpu.roll(packed, (2 * lanes - offset - 2 * (first + step * i)) % lanes, 1) for i in range(count)])


def spread(plane, t, tracers, pair, level):
    moved = pltpu.roll(plane, 2 * t + 1, 1, stride=2 * tracers, stride_axis=0)
    return jnp.sum(jnp.where(pair == level * tracers + t, moved, 0.0), axis=0, keepdims=True)


def from_neighbours(east, west, even_lane):
    return jnp.where(even_lane, pltpu.roll(east, east.shape[1] - 1, 1), pltpu.roll(west, 1, 1))


def face(own, other, even_lane):
    return jnp.where(even_lane, own * (other > 0).astype(F32), other * (own > 0).astype(F32))


def prepare_kernel(tracers, nz, rows, field_in, mask_in, levels_in, east_in, north_in, down_in,
                   field, coef_east, coef_west, coef_north, coef_south, coef_down, east_own, north_own, image, own, message,
                   mask, levels, east, north, down, sems):
    first = nz // 4
    chunks = [(0, first), (first, (nz - first) // 2), (first + (nz - first) // 2, nz - first - (nz - first) // 2)]
    half = first + 1
    pairs = [(mask_in, mask, 0), (east_in, east, 0), (north_in, north, 0), (down_in, down, 0)]
    pairs += [(field_in, field, t * nz) for t in range(tracers)]
    copies = [[(levels_in, levels)], []]
    for part, (start, count) in enumerate(((0, half), (half, nz - half))):
        for a, b, offset in pairs:
            at = pl.ds((offset + start) * rows, count * rows)
            copies[part].append((a.at[at], b.at[at]))
    count = len(copies[0])
    copies = [[pltpu.make_async_copy(a, b, sems.at[i + part * count]) for i, (a, b) in enumerate(copies[part])] for part in range(2)]
    for copy in copies[0] + copies[1]:
        copy.start()
    for copy in copies[0]:
        copy.wait()
    lanes = field.shape[1]
    shape = (1, rows, lanes)
    last_lane, last_row = iota(shape, 2) == lanes - 1, iota(shape, 1) == rows - 1
    first_lane, first_row = iota(shape, 2) == 0, iota(shape, 1) == 0
    pair = iota((rows, lanes), 1) >> 1
    zero = jnp.zeros((rows, lanes), F32)
    packed_image, packed_field, packed_east = zero, zero, zero
    depth = levels[...]
    above = [zero[None]] * tracers
    for k, chunk in chunks:
        if k == first:
            for copy in copies[1]:
                copy.wait()
        level = iota((chunk + 1, rows, lanes), 0)
        count = min(chunk + 1, nz - k)
        wet = (levels_of(mask, k, count, rows) == 1) & (level[:count] + k < depth[None])
        wet = jnp.where(wet, 1.0, 0.0)
        if count == chunk:
            wet = jnp.concatenate([wet, zero[None]], axis=0)
        ocean = wet[:chunk]
        own_east = levels_of(east, k, chunk, rows).astype(F32) * ocean
        own_north = levels_of(north, k, chunk, rows).astype(F32) * ocean
        c_east = jnp.where(last_lane, 0.0, own_east * pltpu.roll(ocean, lanes - 1, 2))
        c_north = jnp.where(last_row, 0.0, own_north * pltpu.roll(ocean, rows - 1, 1))
        c_down = levels_of(down, k, chunk, rows).astype(F32) * ocean * wet[1:]
        c_west = jnp.where(first_lane, 0.0, pltpu.roll(own_east, 1, 2) * ocean)
        c_south = jnp.where(first_row, 0.0, pltpu.roll(own_north, 1, 1) * ocean)
        c = (c_east, c_west, c_north, c_south, c_down)
        packed_east = packed_into(packed_east, own_east, k * tracers, tracers, pair)
        changes = []
        for t in range(tracers):
            value = levels_of(field, t * nz + k, chunk, rows)
            below = levels_of(field, t * nz + k + chunk, 1, rows) if k + chunk < nz else zero[None]
            change, above[t] = laplacian(value, below, above[t], c)
            changes.append(change)
            packed_field = packed_into(packed_field, value, k * tracers + t, tracers, pair)
        for t in range(tracers):
            packed_image = packed_into(packed_image, changes[t], k * tracers + t, tracers, pair)
        for ref, value in zip((coef_east, coef_west, coef_north, coef_south, coef_down, east_own, north_own), c + (own_east, own_north)):
            put_levels(ref, k, value)
        for t in range(tracers):
            put_levels(image, t * nz + k, changes[t])
    own[pl.ds(0, rows), :] = packed_image
    own[pl.ds(rows, rows), :] = packed_field
    own[pl.ds(2 * rows, rows), :] = for_tracers(packed_east, tracers)
    put_message(rows, own, message, True)


def put_message(rows, own, message, second):
    lanes = own.shape[1]
    eastern = is_even("lon") != second
    even_lane = (iota((rows, lanes), 1) & 1) == 0
    image, field = own[pl.ds(0, rows), :], own[pl.ds(rows, rows), :]
    to_east = jnp.where(even_lane, image, pltpu.roll(field, 1, 1))
    to_west = jnp.where(even_lane, pltpu.roll(field, lanes - 1, 1), image)
    message[pl.ds(0, rows), :] = jnp.where(eastern, to_east, to_west)
    message[pl.ds(rows, rows), :] = own[pl.ds(2 * rows, rows), :]


def edge_rows(tracers, nz, rows, field, image, east_own, north_own, second, out):
    southern = is_even("lat") if second else jnp.logical_not(is_even("lat"))

    def edge(side):
        first = (rows - 1) * side
        parts = [ref[pl.ds(first + t * nz * rows, nz, rows), :] for ref in (image, field) for t in range(tracers)]
        return parts + [(east_own, north_own)[side][pl.ds(first, nz, rows), :]]

    for at, (south, north_) in enumerate(zip(edge(0), edge(1))):
        out[pl.ds(at * nz, nz), :] = jnp.where(southern, south, north_)


def edges_kernel(tracers, nz, rows, field, image, east_own, north_own, rows_b):
    edge_rows(tracers, nz, rows, field, image, east_own, north_own, True, rows_b)


def later_kernel(tracers, nz, rows, field, image, east_own, north_own, own, rows_b, rows_a, message_a):
    edge_rows(tracers, nz, rows, field, image, east_own, north_own, False, rows_a)
    put_message(rows, own, message_a, False)


def for_tracers(packed, tracers):
    return sum((pltpu.roll(packed, 2 * t, 1) for t in range(1, tracers)), packed)


def stacked(parts):
    lanes = parts[0].shape[1]
    row = iota((8, lanes), 0)
    total = jnp.zeros((8, lanes), F32)
    for i, part in enumerate(parts):
        total = jnp.where(row == i, part, total)
    return total


def folded(x):
    return sum(x[i : i + 8] for i in range(0, x.shape[0], 8))


def interior_kernel(tracers, nz, rows, field, image, coef_east, coef_west, coef_north, coef_south, coef_down,
                    twice, packed, sums):
    lanes = field.shape[1]
    pair, last_lane = iota((rows, lanes), 1) >> 1, iota((CHUNK, rows, lanes), 2) == lanes - 1
    zero = jnp.zeros((rows, lanes), F32)
    packed_twice, packed_north, packed_down, packed_inner = [zero] * 4
    totals = [[zero] * 4 for _ in range(tracers)]
    above = [zero[None]] * tracers
    for k in range(0, nz, CHUNK):
        refs = (coef_east, coef_west, coef_north, coef_south, coef_down)
        c = [levels_of(ref, k, CHUNK, rows) for ref in refs]
        results = []
        for t in range(tracers):
            w = levels_of(image, t * nz + k, CHUNK, rows)
            below = levels_of(image, t * nz + k + CHUNK, 1, rows) if k + CHUNK < nz else zero[None]
            y, above[t] = laplacian(w, below, above[t], c)
            results.append(y)
            v = levels_of(field, t * nz + k, CHUNK, rows)
            for i, product in enumerate((v * v, v * w, w * w, w * y)):
                totals[t][i] = totals[t][i] + jnp.sum(product, axis=0)
        inner = jnp.where(last_lane, c[1], c[0])
        packed_north = packed_into(packed_north, c[2], k * tracers, tracers, pair)
        packed_down = packed_into(packed_down, c[4], k * tracers, tracers, pair)
        packed_inner = packed_into(packed_inner, inner, k * tracers, tracers, pair)
        for t in range(tracers):
            packed_twice = packed_into(packed_twice, results[t], k * tracers + t, tracers, pair)
        for t in range(tracers):
            put_levels(twice, t * nz + k, results[t])
    packed[pl.ds(0, rows), :] = packed_twice
    for i, part in enumerate((packed_north, packed_down, packed_inner)):
        packed[pl.ds((i + 1) * rows, rows), :] = for_tracers(part, tracers)
    for t in range(tracers):
        for i in range(4):
            sums[pl.ds((4 * t + i) * 8, 8), :] = folded(totals[t][i])


def sums_kernel(tracers, nz, rows, devices, image_in, twice_in, coef_east, coef_north, coef_down, rows_a, rows_b, got_rows_a,
                got_rows_b, own, got_a, got_b, packed, sums, image, twice, corrections, result):
    lanes = own.shape[1]
    even = is_even("lat")
    pair, level = iota((nz, lanes), 1) >> 1, iota((nz, lanes), 0)
    row = iota((rows, lanes), 0)
    north, down, inner = [packed[pl.ds((i + 1) * rows, rows), :] for i in range(3)]
    dots = [[jnp.zeros((8, lanes), F32) for _ in range(3)] for _ in range(tracers)]
    nothing = jnp.zeros((1, lanes), F32)
    row_change, row_inside = jnp.zeros((rows, lanes), F32), jnp.zeros((rows, lanes), F32)
    lat_coef, lat_ring, lat_change = [], [], []
    stores = []
    for side in range(SIDES):
        def part(at, a, b):
            first, second = (b, a) if side == 0 else (a, b)
            return jnp.where(even, first[pl.ds(at * nz, nz), :], second[pl.ds(at * nz, nz), :])

        own_row = lambda at: part(at, rows_a, rows_b)
        got_row = lambda at: part(at, got_rows_a, got_rows_b)
        own_coef, got_coef = own_row(2 * tracers), got_row(2 * tracers)
        c = got_coef * (own_coef > 0).astype(F32) if side == 0 else own_coef * (got_coef > 0).astype(F32)
        c = c * jnp.where(lax.axis_index("lat") == (0, lax.axis_size("lat") - 1)[side], 0.0, 1.0)
        first, next_row, between = ((0, 1, 0), (rows - 1, rows - 2, rows - 2))[side]
        c_east, c_down = coef_east[pl.ds(first, nz, rows), :], coef_down[pl.ds(first, nz, rows), :]
        c_inner = coef_north[pl.ds(between, nz, rows), :]
        packed_coef, packed_ring, packed_e, packed_inside = [nothing] * 4
        for t in range(tracers):
            b, w = own_row(tracers + t), own_row(t)
            f = c * (got_row(tracers + t) - b)
            e = -f
            ring = got_row(t) + f
            flux_east = c_east * (pltpu.roll(e, lanes - 1, 1) - e)
            flux_down = c_down * (pltpu.roll(e, nz - 1, 0) - e)
            inside = (pltpu.roll(flux_east, 1, 1) - flux_east) + (pltpu.roll(flux_down, 1, 0) - flux_down) + c_inner * e
            changed = w + e
            through = c * (ring - changed)
            at = pl.ds(first + t * nz * rows, nz, rows)
            at_next = pl.ds(next_row + t * nz * rows, nz, rows)
            y = twice_in[at, :]
            stores.append((image, at, changed))
            stores.append((twice, at, y + inside - through))
            stores.append((twice, at_next, twice_in[at_next, :] - c_inner * e))
            for i, value in enumerate((b * e, (w + changed) * e, (2.0 * y + inside) * e - changed * through)):
                dots[t][i] = dots[t][i] + folded(value)
            packed_coef = packed_coef + spread(c, t, tracers, pair, level)
            packed_ring = packed_ring + spread(ring, t, tracers, pair, level)
            packed_e = packed_e + spread(e, t, tracers, pair, level)
            packed_inside = packed_inside + spread(inside, t, tracers, pair, level)
        row_change = jnp.where(row == first, packed_e, row_change)
        row_inside = jnp.where(row == first, packed_inside, row_inside)
        row_inside = jnp.where(row == next_row, -north[between : between + 1] * packed_e, row_inside)
        lat_coef.append(packed_coef)
        lat_ring.append(packed_ring)
        lat_change.append(-packed_e)
    for ref, at, value in stores:
        ref[at, :] = value

    even = is_even("lon")
    even_lane = (iota((rows, lanes), 1) & 1) == 0

    def neighbours(at):
        a, b = got_a[at, :], got_b[at, :]
        return jnp.where(even, a, b), jnp.where(even, b, a)

    parts = [pl.ds(i * rows, rows) for i in range(3)]
    own_image, own_field, own_east = [own[p, :] for p in parts]
    columns = neighbours(parts[0])
    got_image, got_field = from_neighbours(*columns, even_lane), jnp.where(even_lane, *columns)
    got_east = from_neighbours(*neighbours(parts[1]), even_lane)
    before = own_image + row_change
    y = packed[pl.ds(0, rows), :] + row_inside
    c = face(own_east, got_east, even_lane)
    f = c * (got_field - own_field)
    e = -f
    after = before + e
    ring = got_image + f
    through = c * (ring - after)
    through_new = through_old = halves = jnp.zeros((rows, lanes), F32)
    for side in range(SIDES):
        here = row == (rows - 1) * side
        through_new = jnp.where(here, lat_coef[side] * (lat_ring[side] - after), through_new)
        through_old = jnp.where(here, lat_coef[side] * (lat_ring[side] - before), through_old)
        halves = jnp.where(here, lat_coef[side] * lat_ring[side] * f + c * ring * lat_change[side], halves)
    flux_down = down * (pltpu.roll(e, lanes - 2 * tracers, 1) - e)
    flux_north = north * (pltpu.roll(e, rows - 1, 0) - e)
    inside = (pltpu.roll(flux_down, 2 * tracers, 1) - flux_down) + (pltpu.roll(flux_north, 1, 0) - flux_north) + inner * e
    beside = -inner * e
    corrections[parts[0], :] = e
    corrections[parts[1], :] = inside - through - (through_new - through_old)
    corrections[parts[2], :] = beside
    edges = [(rows - 1) * side for side in range(SIDES)]
    corrections[pl.ds(3 * rows, 8), :] = stacked(lat_coef + [c[i : i + 1] for i in edges])

    column_dots = [folded(value) for value in (
        own_field * e,
        (before + after) * e,
        (2.0 * y + inside) * e - after * (through + through_new) + before * through_old + halves,
    )]
    tile_lane, tile_row = iota((8, lanes), 1), iota((8, lanes), 0)
    total = jnp.zeros((8, lanes), F32)
    for t in range(tracers):
        mine = lax.rem(tile_lane >> 1, tracers) == t
        for i in range(4):
            value = sums[pl.ds((4 * t + i) * 8, 8), :]
            if i:
                value = value + dots[t][i - 1] + jnp.where(mine, column_dots[i - 1], 0.0)
            total = jnp.where(tile_row == 4 * t + i, jnp.sum(value, axis=0, keepdims=True), total)
    total = jnp.sum(total, axis=1, keepdims=True)
    total = jnp.sum(jnp.where(tile_row == tile_lane, total, 0.0), axis=0, keepdims=True)
    even_row = (iota((1, lanes), 1) & 1) == 0
    south, north_ = edges
    lon_shares = [2.0 * c[i : i + 1] * part for i, part in zip(edges, lat_change)]
    shares = [total, 2.0 * lat_coef[1] * f[north_ : north_ + 1], jnp.where(even_row, lon_shares[0], lat_change[0]),
              jnp.where(even_row, lon_shares[1], f[south : south + 1])]
    for i, share in enumerate(shares):
        result[pl.ds(i, devices, SHARES), :] = jnp.broadcast_to(share, (devices, lanes))


def finish_kernel(tracers, nz, rows, devices, field, image, twice, corrections, sums, solution_out, residual_out,
                  solution, residual, sems):
    lanes = field.shape[1]
    across, along = lax.axis_size("lon"), lax.axis_size("lat")
    one = iota((1, lanes), 1)
    even_one = (one & 1) == 0
    total, to_north, lon_south, mixed = [sums[pl.ds(i, devices, SHARES), :] for i in range(SHARES)]
    total = jnp.sum(total, axis=0, keepdims=True)
    even_lane = (iota((devices, lanes), 1) & 1) == 0
    from_east = lambda x: pltpu.roll(pltpu.roll(x, devices - along, 0), lanes - 1, 1)
    from_north = lambda x: pltpu.roll(x, devices - 1, 0)
    beyond = from_east(lon_south)
    cross = jnp.where(even_lane, lon_south * beyond - mixed * from_north(beyond), 0.0)
    cross = cross + to_north * from_north(jnp.where(even_lane, -from_east(mixed), mixed))
    cross = jnp.sum(cross, axis=0, keepdims=True)

    lon, lat = lax.axis_index("lon"), lax.axis_index("lat")
    share = lambda i, j, at: sums[pl.ds(SHARES * (i * along + j) + at, 1), :]
    faces = corrections[pl.ds(3 * rows, 8), :]
    east, west = lax.rem(lon + 1, across), lax.rem(lon + across - 1, across)
    south, north = jnp.maximum(lat - 1, 0), jnp.minimum(lat + 1, along - 1)
    northern = jnp.where(lat < along - 1, 1.0, 0.0)
    lat_sides = (share(lon, south, 1) * jnp.where(lat > 0, 0.5, 0.0),
                 faces[1:2] * jnp.where(even_one, -pltpu.roll(share(east, north, 3), lanes - 1, 1), share(lon, north, 3)))
    lon_sides = (from_neighbours(share(east, lat, 2), 0.5 * share(west, lat, 2), even_one),
                 from_neighbours(-northern * share(east, north, 2), 0.5 * share(west, lat, 3), even_one))
    sides = [lat_sides[i] + jnp.where(even_one, faces[2 + i : 3 + i] * lon_sides[i], lon_sides[i]) for i in range(SIDES)]
    row = iota((rows, lanes), 0)
    e, change, beside = [corrections[pl.ds(i * rows, rows), :] for i in range(3)]
    change = change + jnp.where(row == 0, sides[0], jnp.where(row == rows - 1, sides[1], 0.0))

    lane = iota((CHUNK, rows, lanes), 2)
    narrow = iota((rows, lanes), 1)
    edge = (lane == 0) | (lane == lanes - 1)
    near = (lane <= 1) | (lane >= lanes - 2)

    def number(i):
        return jnp.sum(jnp.where(one == i, total, 0.0), axis=1, keepdims=True)

    copies = []
    for t in range(tracers):
        bb, bw, ww, wy = [number(4 * t + i) for i in range(4)]
        mine = lax.rem(one >> 1, tracers) == t
        wy = wy - jnp.sum(jnp.where(mine, cross, 0.0), axis=1, keepdims=True)
        whole = 1.0 / (bb + bw)
        step = bb * whole
        rest = bw * whole
        beta = step * (ww * whole) - rest * rest
        new = beta * bb
        tau = beta + rest
        step_next = new / (new + beta * new + tau * tau * bw - 2.0 * tau * step * ww + step * step * wy)
        both = step * step_next
        s_b = step + step_next * tau
        r_b = rest - step_next * tau
        r_w = both - step - step_next * tau
        s_edge = -both * e
        r_edge = jnp.where(lax.rem(narrow >> 1, tracers) == t, r_w * e + both * change,
                           both * jnp.where((narrow & 1) == 0, pltpu.roll(beside, 1, 1), pltpu.roll(beside, lanes - 1, 1)))
        for k in range(0, nz, CHUNK):
            slot, first = t * nz + k, k * tracers + t
            v, w, y = [levels_of(ref, slot, CHUNK, rows) for ref in (field, image, twice)]
            more = jnp.where(edge, unpacked(s_edge, first, tracers, CHUNK), 0.0)
            much = jnp.where(near, unpacked(r_edge, first, tracers, CHUNK), 0.0)
            put_levels(solution, slot, (s_b * v - both * w) + more)
            put_levels(residual, slot, (r_b * v + r_w * w + both * y) + much)
            at = pl.ds(slot * rows, CHUNK * rows)
            for a, b in ((solution, solution_out), (residual, residual_out)):
                copy = pltpu.make_async_copy(a.at[at], b.at[at], sems.at[len(copies)])
                copy.start()
                copies.append(copy)
    for copy in copies:
        copy.wait()


def swapped(x, axis, second):
    devices = lax.axis_size(axis)
    forward = [(i % 2 == 0) != second for i in range(devices)]
    return lax.ppermute(x, axis, [(i, (i + 1 if forward[i] else i - 1) % devices) for i in range(devices)])


def body(right_side, sea_mask, levels, east_diffusivity, north_diffusivity, vertical_diffusivity):
    tracers, nz, rows, lanes = right_side.shape
    devices = lax.axis_size("lon") * lax.axis_size("lat")
    flat = lambda x: x.reshape(-1, lanes)
    outside = lambda x: pltpu.with_memory_space_constraint(flat(x), pltpu.HBM)
    n = nz * rows
    cells = tracers * n * lanes

    def call(kernel, outs, flops, space=pltpu.VMEM, **more):
        cost = pl.CostEstimate(flops=flops, bytes_accessed=4 * lanes * sum(outs), transcendentals=0)
        return pl.pallas_call(
            functools.partial(kernel, tracers, nz, rows),
            out_shape=[space((m, lanes), F32) for m in outs],
            compiler_params=pltpu.CompilerParams(vmem_limit_bytes=32 * 1024 * 1024),
            cost_estimate=cost,
            **more,
        )

    def with_devices(kernel):
        return lambda tracers, nz, rows, *refs: kernel(tracers, nz, rows, devices, *refs)

    scratch = lambda m, dtype: pltpu.VMEM((m, lanes), dtype)
    field, coef_east, coef_west, coef_north, coef_south, coef_down, east_own, north_own, image, own, message = call(
        prepare_kernel,
        [tracers * n] + [n] * 7 + [tracers * n, 3 * rows, 2 * rows],
        60 * cells,
        in_specs=[pl.BlockSpec(memory_space=pltpu.HBM)] * 6,
        scratch_shapes=[scratch(n, jnp.int32), scratch(rows, jnp.int32)] + [scratch(n, jnp.bfloat16)] * 3
        + [pltpu.SemaphoreType.DMA((9 + 2 * tracers,))],
        name="prepare",
    )(*map(outside, (right_side, sea_mask, levels, east_diffusivity, north_diffusivity, vertical_diffusivity)))
    got_b = swapped(message, "lon", True)
    rows_b, = call(edges_kernel, [FIELDS * nz], cells, name="edges")(field, image, east_own, north_own)
    got_rows_b = swapped(rows_b, "lat", True)
    coefs = (coef_east, coef_west, coef_north, coef_south, coef_down)
    rows_a, message_a = call(later_kernel, [FIELDS * nz, 2 * rows], cells, name="later")(
        field, image, east_own, north_own, own, rows_b)
    twice, packed, sums = call(
        interior_kernel, [tracers * n, 4 * rows, 8 * 4 * tracers], 60000 * cells, name="interior"
    )(field, image, *coefs)
    got_a = swapped(message_a, "lon", False)
    got_rows_a = swapped(rows_a, "lat", False)
    image, twice, corrections, sums = call(
        with_devices(sums_kernel), [tracers * n, tracers * n, 3 * rows + 8, SHARES * devices], cells,
        input_output_aliases={0: 0, 1: 1}, name="sums",
    )(image, twice, coef_east, coef_north, coef_down, rows_a, rows_b, got_rows_a, got_rows_b, own, got_a, got_b, packed, sums)
    sums = lax.all_to_all(sums.reshape(devices, 1, -1), ("lon", "lat"), 0, 0, tiled=True).reshape(-1, lanes)
    copies = 2 * tracers * nz // CHUNK
    solution_field, residual = call(
        with_devices(finish_kernel), [tracers * n] * 2, 20 * cells, space=jax.ShapeDtypeStruct,
        out_specs=[pl.BlockSpec(memory_space=pltpu.HBM)] * 2,
        scratch_shapes=[scratch(tracers * n, F32)] * 2 + [pltpu.SemaphoreType.DMA((copies,))],
        name="finish",
    )(field, image, twice, corrections, sums)
    return solution_field.reshape(right_side.shape), residual.reshape(right_side.shape)


def solution(mesh):
    return jax.shard_map(
        body,
        mesh=mesh,
        in_specs=(
            P(None, None, "lat", "lon"),
            P(None, "lat", "lon"),
            P("lat", "lon"),
            P(None, "lat", "lon"),
            P(None, "lat", "lon"),
            P(None, "lat", "lon"),
        ),
        out_specs=(P(None, None, "lat", "lon"), P(None, None, "lat", "lon")),
        check_vma=False,
    )
```

profile of v0, /device:TPU:0, one launch (start us, length us, event | category | flops | bytes accessed | tf_op | source)
XLA Modules:
  0.0 25.7 jit_solution(3717244654493371563)
XLA Ops:
  0.6 2.1 %prepare.1 = (f32[1024,128]{1,0:T(8,128)S(1)}, f32[512,128]{1,0:T(8,128)S(1)}, f32[512,128]{1,0:T(8,128)S(1)}, f32[512,128]{1,0:T(8,128)S(1)}, f32[512,128]{1,0:...) custom-call(f32[1024,128]{1,0:T(8,128)} %bitcast.11, ...), custom_call_target="tpu_custom_call" | custom-call | flops 7864320 | bytes 2924544 | tf_op jit(solution)/shard_map/prepare/pallas_call | solution.py:442
  2.8 6.0 %collective-permute-start.3 = (f32[32,128]{1,0:T(8,128)S(1)}, f32[32,128]{1,0:T(8,128)S(1)}, u32[]{:S(2)}, u32[]{:S(2)}) collective-permute-start(f32[32,128]{1,0:T(8,128)S(1)} %get-tuple-element.37), channel_id=1, source_target_pairs={{0,28},{4,8},{8,4},{12,16},{16,12},{20,24},{24,20},{28,0},{1,29},{... | collective-permute-start | bytes 49160 | tf_op jit(solution)/shard_map/ppermute | solution.py:417
  8.8 0.1 edges.1.rows_b.refs_6_
  8.9 0.7 %collective-permute-start.1 = (f32[160,128]{1,0:T(8,128)S(1)}, f32[160,128]{1,0:T(8,128)S(1)}, u32[]{:S(2)}, u32[]{:S(2)}) collective-permute-start(f32[160,128]{1,0:T(8,128)S(1)} %edges.1.rows_b.refs_6_), channel_id=1, source_target_pairs={{0,3},{1,2},{2,1},{3,0},{4,7},{5,6},{6,5},{7,4},{8,11},{9,10},{10,... | collective-permute-start | bytes 245768 | tf_op jit(solution)/shard_map/ppermute | solution.py:417
  9.6 0.1 later.1
  9.7 0.1 collective-permute-start.2
  9.8 1.0 %collective-permute-start = (f32[160,128]{1,0:T(8,128)S(1)}, f32[160,128]{1,0:T(8,128)S(1)}, u32[]{:S(2)}, u32[]{:S(2)}) collective-permute-start(f32[160,128]{1,0:T(8,128)S(1)} %get-tuple-element.35.refs_5_), channel_id=1, source_target_pairs={{0,1},{1,0},{2,3},{3,2},{4,5},{5,4},{6,7},{7,6},{8,9},{9,8},{10,11... | collective-permute-start | bytes 245768 | tf_op jit(solution)/shard_map/ppermute | solution.py:417
  10.8 0.8 %interior.1 = (f32[1024,128]{1,0:T(8,128)S(1)}, f32[64,128]{1,0:T(8,128)S(1)}, f32[64,128]{1,0:T(8,128)S(1)}) custom-call(f32[1024,128]{1,0:T(8,128)S(1)} %get-tuple-element.24.field.refs_0_, f32[1024,128]{1,0:T(8,128)S(1)} %get-tuple-element.25.image.refs_0_, f32[512,128]{1,0:T(8,128)S(1)} %get-tuple-element.26.coef_east.refs_2_, ...), custom_call_target="tpu_custom_call" | custom-call | flops 7864320000 | bytes 589824 | tf_op jit(solution)/shard_map/interior/pallas_call | solution.py:457
  11.6 0.0 collective-permute-done.3.refs_11_
  11.6 2.1 %collective-permute-done.2.refs_10_ = f32[32,128]{1,0:T(8,128)S(1)} collective-permute-done((f32[32,128]{1,0:T(8,128)S(1)}, f32[32,128]{1,0:T(8,128)S(1)}, u32[]{:S(2)}, u32[]{:S(2)}) %collective-permute-start.2) | collective-permute-done | bytes 16416 | tf_op jit(solution)/shard_map/ppermute | solution.py:417
  13.6 0.0 collective-permute-done.refs_7_
  13.6 0.0 collective-permute-done.1.refs_8_
  13.6 0.4 %sums.1 = (f32[1024,128]{1,0:T(8,128)S(1)}, f32[1024,128]{1,0:T(8,128)S(1)}, f32[56,128]{1,0:T(8,128)S(1)}, f32[128,128]{1,0:T(8,128)S(1)}) custom-call(f32[1024,128]{1,0:T(8,128)S(1)} %get-tuple-element.25.image.refs_0_, f32[1024,128]{1,0:T(8,128)S(1)} %get-tuple-element.31.refs_1_, ...), custom_call_target="tpu_custom_call", output_to_operand_aliasing={{0}: (0, {}), {1}: (1, {})} | custom-call | flops 131072 | bytes 1142784 | tf_op jit(solution)/shard_map/sums/pallas_call | solution.py:462
  14.1 10.1 %all_to_all.5 = f32[32,1,512]{2,1,0:T(1,128)S(1)} all-to-all(f32[32,1,512]{2,1,0:T(1,128)S(1)} %bitcast.10), channel_id=1, replica_groups=mesh['lon'=8,'lat'=4] {'lon','lat'}, dimensions={0} | all-to-all | bytes 131072 | tf_op jit(solution)/shard_map/all_to_all | solution.py:466
  24.2 1.4 %finish.1 = (f32[1024,128]{1,0:T(8,128)}, f32[1024,128]{1,0:T(8,128)}) custom-call(f32[1024,128]{1,0:T(8,128)S(1)} %get-tuple-element.24.field.refs_0_, f32[1024,128]{1,0:T(8,128)S(1)} %get-tuple-element.40.refs_1_, f32[1024,128]{1,0:T(8,128)S(1)} %get-tuple-element.41.refs_2_, f32[56,128]{1,0:T(8,128)S(1)} %get-tuple-element.42.refs_3_, f32[128,128]{1,0:T(8,128)S(1)} %bitcast.9), custom_call_target="tpu_custom_call" | custom-call | flops 2621440 | bytes 1048576 | tf_op jit(solution)/shard_map/finish/pallas_call | solution.py:468
Async XLA Ops:
  2.8 8.8 %collective-permute-start.3 = (f32[32,128]{1,0:T(8,128)S(1)}, f32[32,128]{1,0:T(8,128)S(1)}, u32[]{:S(2)}, u32[]{:S(2)}) collective-permute-start(f32[32,128]{1,0:T(8,128)S(1)} %get-tuple-element.37), channel_id=1, source_target_pairs={{0,28},{4,8},{8,4},{12,16},{16,12},{20,24},{24,20},{28,0},{1,29},{... | collective-permute-start | bytes 49160 | tf_op jit(solution)/shard_map/ppermute | solution.py:417
  8.9 4.8 %collective-permute-start.1 = (f32[160,128]{1,0:T(8,128)S(1)}, f32[160,128]{1,0:T(8,128)S(1)}, u32[]{:S(2)}, u32[]{:S(2)}) collective-permute-start(f32[160,128]{1,0:T(8,128)S(1)} %edges.1.rows_b.refs_6_), channel_id=1, source_target_pairs={{0,3},{1,2},{2,1},{3,0},{4,7},{5,6},{6,5},{7,4},{8,11},{9,10},{10,... | collective-permute-start | bytes 245768 | tf_op jit(solution)/shard_map/ppermute | solution.py:417
  9.7 4.0 %collective-permute-start.2 = (f32[32,128]{1,0:T(8,128)S(1)}, f32[32,128]{1,0:T(8,128)S(1)}, u32[]{:S(2)}, u32[]{:S(2)}) collective-permute-start(f32[32,128]{1,0:T(8,128)S(1)} %get-tuple-element.36), channel_id=1, source_target_pairs={{0,4},{4,0},{8,12},{12,8},{16,20},{20,16},{24,28},{28,24},{1,5},{5... | collective-permute-start | bytes 49160 | tf_op jit(solution)/shard_map/ppermute | solution.py:417
  9.8 3.9 %collective-permute-start = (f32[160,128]{1,0:T(8,128)S(1)}, f32[160,128]{1,0:T(8,128)S(1)}, u32[]{:S(2)}, u32[]{:S(2)}) collective-permute-start(f32[160,128]{1,0:T(8,128)S(1)} %get-tuple-element.35.refs_5_), channel_id=1, source_target_pairs={{0,1},{1,0},{2,3},{3,2},{4,5},{5,4},{6,7},{7,6},{8,9},{9,8},{10,11... | collective-permute-start | bytes 245768 | tf_op jit(solution)/shard_map/ppermute | solution.py:417
where the time goes:
time: 25.9 us; the launch traced here: 25.7 us
  blocking collectives  10.1 us (39%)
  starting transfers between devices  7.87 us (30%)
  Pallas kernels  4.93 us (19%)
  waiting for transfers between devices  2.06 us (8%)
  between operations  0.67 us (3%)
    all_to_all x1, blocking collectives, body(): lax.all_to_all(sums.reshape(devices, 1, -1), ('lon', 'lat'), 0, 0, tiled=...  10.1 us
    ppermute x4, starting transfers between devices, swapped(): lax.ppermute(x, axis, [(i, (i + 1 if forward[i] else i - 1) % devices) fo...  7.87 us
    pallas_call x1, Pallas kernels, body(): call(prepare_kernel, [tracers * n] + [n] * 7 + [tracers * n, 3 * rows, 2...  2.13 us
    ppermute x4, waiting for transfers between devices, swapped(): lax.ppermute(x, axis, [(i, (i + 1 if forward[i] else i - 1) % devices) fo...  2.06 us
    pallas_call x1, Pallas kernels, body(): call(with_devices(finish_kernel), [tracers * n] * 2, 20 * cells, space=ja...  1.44 us
    pallas_call x1, Pallas kernels, body(): call(interior_kernel, [tracers * n, 4 * rows, 8 * 4 * tracers], 60000 * c...  0.8 us
  transfers between devices with their start and end apart: 4, of which 1 were waited for; matrix products, arithmetic and copies ran while one was open for 0% of the time, Pallas kernels for 4%

commit v1 on v0

--- a/solution.py
+++ b/solution.py
@@ -59,6 +59,18 @@
     return jnp.sum(jnp.where(pair == level * tracers + t, moved, 0.0), axis=0, keepdims=True)
 
 
+def fours_into(total, planes, first, four):
+    moved = [pltpu.roll(planes[i], 4 * (first + i) + 2, 1) for i in range(planes.shape[0])]
+    for i, plane in enumerate(moved):
+        total = jnp.where(four == first + i, plane, total)
+    return total
+
+
+def pairs_of(fours, lane):
+    lanes = lane.shape[1]
+    return jnp.where((lane & 2) == 0, pltpu.roll(fours[0], lanes - 1, 1), pltpu.roll(fours[1], 1, 1))
+
+
 def from_neighbours(east, west, even_lane):
     return jnp.where(even_lane, pltpu.roll(east, east.shape[1] - 1, 1), pltpu.roll(west, 1, 1))
 
@@ -67,39 +79,64 @@
     return jnp.where(even_lane, own * (other > 0).astype(F32), other * (own > 0).astype(F32))
 
 
-def prepare_kernel(tracers, nz, rows, field_in, mask_in, levels_in, east_in, north_in, down_in,
-                   field, coef_east, coef_west, coef_north, coef_south, coef_down, east_own, north_own, image, own, message,
-                   mask, levels, east, north, down, sems):
-    first = nz // 4
-    chunks = [(0, first), (first, (nz - first) // 2), (first + (nz - first) // 2, nz - first - (nz - first) // 2)]
-    half = first + 1
-    pairs = [(mask_in, mask, 0), (east_in, east, 0), (north_in, north, 0), (down_in, down, 0)]
-    pairs += [(field_in, field, t * nz) for t in range(tracers)]
-    copies = [[(levels_in, levels)], []]
-    for part, (start, count) in enumerate(((0, half), (half, nz - half))):
-        for a, b, offset in pairs:
-            at = pl.ds((offset + start) * rows, count * rows)
-            copies[part].append((a.at[at], b.at[at]))
-    count = len(copies[0])
-    copies = [[pltpu.make_async_copy(a, b, sems.at[i + part * count]) for i, (a, b) in enumerate(copies[part])] for part in range(2)]
-    for copy in copies[0] + copies[1]:
+def columns_kernel(tracers, nz, rows, field_in, mask_in, levels_in, east_in, north_in, down_in,
+                   field, mask, levels, east, north, down, own, message, packed, sems):
+    pairs = ((levels_in, levels), (mask_in, mask), (field_in, field), (east_in, east), (north_in, north), (down_in, down))
+    copies = [pltpu.make_async_copy(a, b, sems.at[i]) for i, (a, b) in enumerate(pairs)]
+    for copy in copies:
         copy.start()
-    for copy in copies[0]:
+    lanes = field.shape[1]
+    lane, row = iota((rows, lanes), 1), iota((rows, lanes), 0)
+    four, place = lane >> 2, lane & 3
+    zero = jnp.zeros((rows, lanes), F32)
+    chunk = nz // 2
+
+    def fours_of(ref, start=0, see=lambda value, k: value.astype(F32)):
+        total = zero
+        for k in range(0, nz, chunk):
+            total = fours_into(total, see(levels_of(ref, start + k, chunk, rows), k), k, four)
+        return total
+
+    for copy in copies[:3]:
         copy.wait()
+    depth = levels[...]
+    level = iota((chunk, rows, lanes), 0)
+    wet = fours_of(mask, see=lambda value, k: jnp.where((value == 1) & (level + k < depth[None]), 1.0, 0.0))
+    fields = [fours_of(field, t * nz) for t in range(tracers)]
+    for copy in copies[3:]:
+        copy.wait()
+    wide_east, wide_north, wide_down = fours_of(east), fours_of(north), fours_of(down)
+    own_east = wide_east * wet
+    inner = own_east * pltpu.roll(wet, lanes - 1, 1)
+    inner = jnp.where(place == 1, pltpu.roll(inner, 1, 1), inner)
+    c_north = jnp.where(row == rows - 1, 0.0, wide_north * wet * pltpu.roll(wet, rows - 1, 0))
+    c_south = pltpu.roll(c_north, 1, 0)
+    c_down = jnp.where(four == nz - 1, 0.0, wide_down * wet * pltpu.roll(wet, lanes - 4, 1))
+    images = []
+    for v in fields:
+        beside = jnp.where(place == 1, pltpu.roll(v, 1, 1), pltpu.roll(v, lanes - 1, 1))
+        flux_down = c_down * (pltpu.roll(v, lanes - 4, 1) - v)
+        change = inner * (v - beside) + c_north * (v - pltpu.roll(v, rows - 1, 0)) + c_south * (v - pltpu.roll(v, 1, 0))
+        images.append(change + (pltpu.roll(flux_down, 4, 1) - flux_down))
+    for i, parts in enumerate((images, fields, (own_east, own_east))):
+        own[pl.ds(i * rows, rows), :] = pairs_of(parts, lane)
+    put_message(rows, own, message, True)
+    for i, part in enumerate((c_north, c_down, inner)):
+        packed[pl.ds(i * rows, rows), :] = pairs_of((part, part), lane)
+
+
+def block_kernel(tracers, nz, rows, field, mask, levels, east, north, down,
+                 coef_east, coef_west, coef_north, coef_south, coef_down, east_own, north_own, image, rows_b):
     lanes = field.shape[1]
+    chunk = nz // 2
     shape = (1, rows, lanes)
     last_lane, last_row = iota(shape, 2) == lanes - 1, iota(shape, 1) == rows - 1
     first_lane, first_row = iota(shape, 2) == 0, iota(shape, 1) == 0
-    pair = iota((rows, lanes), 1) >> 1
     zero = jnp.zeros((rows, lanes), F32)
-    packed_image, packed_field, packed_east = zero, zero, zero
     depth = levels[...]
+    level = iota((chunk + 1, rows, lanes), 0)
     above = [zero[None]] * tracers
-    for k, chunk in chunks:
-        if k == first:
-            for copy in copies[1]:
-                copy.wait()
-        level = iota((chunk + 1, rows, lanes), 0)
+    for k in range(0, nz, chunk):
         count = min(chunk + 1, nz - k)
         wet = (levels_of(mask, k, count, rows) == 1) & (level[:count] + k < depth[None])
         wet = jnp.where(wet, 1.0, 0.0)
@@ -114,24 +151,17 @@
         c_west = jnp.where(first_lane, 0.0, pltpu.roll(own_east, 1, 2) * ocean)
         c_south = jnp.where(first_row, 0.0, pltpu.roll(own_north, 1, 1) * ocean)
         c = (c_east, c_west, c_north, c_south, c_down)
-        packed_east = packed_into(packed_east, own_east, k * tracers, tracers, pair)
         changes = []
         for t in range(tracers):
             value = levels_of(field, t * nz + k, chunk, rows)
             below = levels_of(field, t * nz + k + chunk, 1, rows) if k + chunk < nz else zero[None]
             change, above[t] = laplacian(value, below, above[t], c)
             changes.append(change)
-            packed_field = packed_into(packed_field, value, k * tracers + t, tracers, pair)
-        for t in range(tracers):
-            packed_image = packed_into(packed_image, changes[t], k * tracers + t, tracers, pair)
         for ref, value in zip((coef_east, coef_west, coef_north, coef_south, coef_down, east_own, north_own), c + (own_east, own_north)):
             put_levels(ref, k, value)
         for t in range(tracers):
             put_levels(image, t * nz + k, changes[t])
-    own[pl.ds(0, rows), :] = packed_image
-    own[pl.ds(rows, rows), :] = packed_field
-    own[pl.ds(2 * rows, rows), :] = for_tracers(packed_east, tracers)
-    put_message(rows, own, message, True)
+    edge_rows(tracers, nz, rows, field, image, east_own, north_own, True, rows_b)
 
 
 def put_message(rows, own, message, second):
@@ -157,17 +187,9 @@
         out[pl.ds(at * nz, nz), :] = jnp.where(southern, south, north_)
 
 
-def edges_kernel(tracers, nz, rows, field, image, east_own, north_own, rows_b):
-    edge_rows(tracers, nz, rows, field, image, east_own, north_own, True, rows_b)
-
-
 def later_kernel(tracers, nz, rows, field, image, east_own, north_own, own, rows_b, rows_a, message_a):
     edge_rows(tracers, nz, rows, field, image, east_own, north_own, False, rows_a)
     put_message(rows, own, message_a, False)
-
-
-def for_tracers(packed, tracers):
-    return sum((pltpu.roll(packed, 2 * t, 1) for t in range(1, tracers)), packed)
 
 
 def stacked(parts):
@@ -186,9 +208,8 @@
 def interior_kernel(tracers, nz, rows, field, image, coef_east, coef_west, coef_north, coef_south, coef_down,
                     twice, packed, sums):
     lanes = field.shape[1]
-    pair, last_lane = iota((rows, lanes), 1) >> 1, iota((CHUNK, rows, lanes), 2) == lanes - 1
-    zero = jnp.zeros((rows, lanes), F32)
-    packed_twice, packed_north, packed_down, packed_inner = [zero] * 4
+    pair = iota((rows, lanes), 1) >> 1
+    zero = packed_twice = jnp.zeros((rows, lanes), F32)
     totals = [[zero] * 4 for _ in range(tracers)]
     above = [zero[None]] * tracers
     for k in range(0, nz, CHUNK):
@@ -203,29 +224,23 @@
             v = levels_of(field, t * nz + k, CHUNK, rows)
             for i, product in enumerate((v * v, v * w, w * w, w * y)):
                 totals[t][i] = totals[t][i] + jnp.sum(product, axis=0)
-        inner = jnp.where(last_lane, c[1], c[0])
-        packed_north = packed_into(packed_north, c[2], k * tracers, tracers, pair)
-        packed_down = packed_into(packed_down, c[4], k * tracers, tracers, pair)
-        packed_inner = packed_into(packed_inner, inner, k * tracers, tracers, pair)
         for t in range(tracers):
             packed_twice = packed_into(packed_twice, results[t], k * tracers + t, tracers, pair)
         for t in range(tracers):
             put_levels(twice, t * nz + k, results[t])
-    packed[pl.ds(0, rows), :] = packed_twice
-    for i, part in enumerate((packed_north, packed_down, packed_inner)):
-        packed[pl.ds((i + 1) * rows, rows), :] = for_tracers(part, tracers)
+    packed[...] = packed_twice
     for t in range(tracers):
         for i in range(4):
             sums[pl.ds((4 * t + i) * 8, 8), :] = folded(totals[t][i])
 
 
 def sums_kernel(tracers, nz, rows, devices, image_in, twice_in, coef_east, coef_north, coef_down, rows_a, rows_b, got_rows_a,
-                got_rows_b, own, got_a, got_b, packed, sums, image, twice, corrections, result):
+                got_rows_b, own, got_a, got_b, packed, packed_twice, sums, image, twice, corrections, result):
     lanes = own.shape[1]
     even = is_even("lat")
     pair, level = iota((nz, lanes), 1) >> 1, iota((nz, lanes), 0)
     row = iota((rows, lanes), 0)
-    north, down, inner = [packed[pl.ds((i + 1) * rows, rows), :] for i in range(3)]
+    north, down, inner = [packed[pl.ds(i * rows, rows), :] for i in range(3)]
     dots = [[jnp.zeros((8, lanes), F32) for _ in range(3)] for _ in range(tracers)]
     nothing = jnp.zeros((1, lanes), F32)
     row_change, row_inside = jnp.zeros((rows, lanes), F32), jnp.zeros((rows, lanes), F32)
@@ -289,7 +304,7 @@
     got_image, got_field = from_neighbours(*columns, even_lane), jnp.where(even_lane, *columns)
     got_east = from_neighbours(*neighbours(parts[1]), even_lane)
     before = own_image + row_change
-    y = packed[pl.ds(0, rows), :] + row_inside
+    y = packed_twice[...] + row_inside
     c = face(own_east, got_east, even_lane)
     f = c * (got_field - own_field)
     e = -f
@@ -426,10 +441,11 @@
     cells = tracers * n * lanes
 
     def call(kernel, outs, flops, space=pltpu.VMEM, **more):
-        cost = pl.CostEstimate(flops=flops, bytes_accessed=4 * lanes * sum(outs), transcendentals=0)
+        outs = [m if isinstance(m, tuple) else (m, F32) for m in outs]
+        cost = pl.CostEstimate(flops=flops, bytes_accessed=4 * lanes * sum(m for m, _ in outs), transcendentals=0)
         return pl.pallas_call(
             functools.partial(kernel, tracers, nz, rows),
-            out_shape=[space((m, lanes), F32) for m in outs],
+            out_shape=[space((m, lanes), dtype) for m, dtype in outs],
             compiler_params=pltpu.CompilerParams(vmem_limit_bytes=32 * 1024 * 1024),
             cost_estimate=cost,
             **more,
@@ -439,30 +455,31 @@
         return lambda tracers, nz, rows, *refs: kernel(tracers, nz, rows, devices, *refs)
 
     scratch = lambda m, dtype: pltpu.VMEM((m, lanes), dtype)
-    field, coef_east, coef_west, coef_north, coef_south, coef_down, east_own, north_own, image, own, message = call(
-        prepare_kernel,
-        [tracers * n] + [n] * 7 + [tracers * n, 3 * rows, 2 * rows],
-        60 * cells,
+    *inputs, own, message, packed = call(
+        columns_kernel,
+        [tracers * n, (n, jnp.int32), (rows, jnp.int32)] + [(n, jnp.bfloat16)] * 3 + [3 * rows, 2 * rows, 3 * rows],
+        20 * cells,
         in_specs=[pl.BlockSpec(memory_space=pltpu.HBM)] * 6,
-        scratch_shapes=[scratch(n, jnp.int32), scratch(rows, jnp.int32)] + [scratch(n, jnp.bfloat16)] * 3
-        + [pltpu.SemaphoreType.DMA((9 + 2 * tracers,))],
-        name="prepare",
+        scratch_shapes=[pltpu.SemaphoreType.DMA((6,))],
+        name="columns",
     )(*map(outside, (right_side, sea_mask, levels, east_diffusivity, north_diffusivity, vertical_diffusivity)))
+    field = inputs[0]
     got_b = swapped(message, "lon", True)
-    rows_b, = call(edges_kernel, [FIELDS * nz], cells, name="edges")(field, image, east_own, north_own)
+    coef_east, coef_west, coef_north, coef_south, coef_down, east_own, north_own, image, rows_b = call(
+        block_kernel, [n] * 7 + [tracers * n, FIELDS * nz], 20 * cells, name="block")(*inputs)
     got_rows_b = swapped(rows_b, "lat", True)
     coefs = (coef_east, coef_west, coef_north, coef_south, coef_down)
     rows_a, message_a = call(later_kernel, [FIELDS * nz, 2 * rows], cells, name="later")(
         field, image, east_own, north_own, own, rows_b)
-    twice, packed, sums = call(
-        interior_kernel, [tracers * n, 4 * rows, 8 * 4 * tracers], 60000 * cells, name="interior"
+    twice, packed_twice, sums = call(
+        interior_kernel, [tracers * n, rows, 8 * 4 * tracers], 60000 * cells, name="interior"
     )(field, image, *coefs)
     got_a = swapped(message_a, "lon", False)
     got_rows_a = swapped(rows_a, "lat", False)
     image, twice, corrections, sums = call(
         with_devices(sums_kernel), [tracers * n, tracers * n, 3 * rows + 8, SHARES * devices], cells,
         input_output_aliases={0: 0, 1: 1}, name="sums",
-    )(image, twice, coef_east, coef_north, coef_down, rows_a, rows_b, got_rows_a, got_rows_b, own, got_a, got_b, packed, sums)
+    )(image, twice, coef_east, coef_north, coef_down, rows_a, rows_b, got_rows_a, got_rows_b, own, got_a, got_b, packed, packed_twice, sums)
     sums = lax.all_to_all(sums.reshape(devices, 1, -1), ("lon", "lat"), 0, 0, tiled=True).reshape(-1, lanes)
     copies = 2 * tracers * nz // CHUNK
     solution_field, residual = call(

time: 25.9 us -> 25.5 us (0.985)
  blocking collectives: 10.1 us -> 9.52 us
    all_to_all x1, blocking collectives: 10.1 us -> 9.52 us  [body(): lax.all_to_all(sums.reshape(devices, 1, -1), ('lon', 'lat'), 0, 0, tiled=...]
  transfers between devices with their start and end apart: 4 -> 4, of which waited for: 1 -> 1; matrix products, arithmetic and copies ran while one was open for 0% -> 0% of each run, Pallas kernels for 4% -> 6%
where the time goes in v1:
time: 25.5 us; the launch traced here: 25.3 us
  blocking collectives  9.52 us (37%)
  starting transfers between devices  7.87 us (31%)
  Pallas kernels  5.14 us (20%)
  waiting for transfers between devices  2.12 us (8%)
  between operations  0.66 us (3%)
    all_to_all x1, blocking collectives, body(): lax.all_to_all(sums.reshape(devices, 1, -1), ('lon', 'lat'), 0, 0, tiled=...  9.52 us
    ppermute x4, starting transfers between devices, swapped(): lax.ppermute(x, axis, [(i, (i + 1 if forward[i] else i - 1) % devices) fo...  7.87 us
    ppermute x4, waiting for transfers between devices, swapped(): lax.ppermute(x, axis, [(i, (i + 1 if forward[i] else i - 1) % devices) fo...  2.12 us
    pallas_call x1, Pallas kernels, body(): call(columns_kernel, [tracers * n, (n, jnp.int32), (rows, jnp.int32)] + [...  1.76 us
    pallas_call x1, Pallas kernels, body(): call(with_devices(finish_kernel), [tracers * n] * 2, 20 * cells, space=ja...  1.44 us
    pallas_call x1, Pallas kernels, body(): call(interior_kernel, [tracers * n, rows, 8 * 4 * tracers], 60000 * cells...  0.75 us
    pallas_call x1, Pallas kernels, body(): call(block_kernel, [n] * 7 + [tracers * n, FIELDS * nz], 20 * cells, name...  0.69 us
  transfers between devices with their start and end apart: 4, of which 1 were waited for; matrix products, arithmetic and copies ran while one was open for 0% of the time, Pallas kernels for 6%

profile of v1, /device:TPU:0, one launch (start us, length us, event | category | flops | bytes accessed | tf_op | source)
XLA Modules:
  0.0 25.3 jit_solution(10154587371047861459)
XLA Ops:
  0.6 1.8 %columns.1 = (f32[1024,128]{1,0:T(8,128)S(1)}, s32[512,128]{1,0:T(8,128)S(1)}, s32[16,128]{1,0:T(8,128)S(1)}, bf16[512,128]{1,0:T(8,128)(2,1)S(1)}, bf16[512,128...) custom-call(f32[1024,128]{1,0:T(8,128)} %bitcast.11, ...), custom_call_target="tpu_custom_call" | custom-call | flops 2621440 | bytes 1646592 | tf_op jit(solution)/shard_map/columns/pallas_call | solution.py:458
  2.4 6.0 %collective-permute-start.3 = (f32[32,128]{1,0:T(8,128)S(1)}, f32[32,128]{1,0:T(8,128)S(1)}, u32[]{:S(2)}, u32[]{:S(2)}) collective-permute-start(f32[32,128]{1,0:T(8,128)S(1)} %get-tuple-element.50), channel_id=1, source_target_pairs={{0,28},{4,8},{8,4},{12,16},{16,12},{20,24},{24,20},{28,0},{1,29},{... | collective-permute-start | bytes 49160 | tf_op jit(solution)/shard_map/ppermute | solution.py:432
  8.4 0.7 %block.1 = (f32[512,128]{1,0:T(8,128)S(1)}, f32[512,128]{1,0:T(8,128)S(1)}, f32[512,128]{1,0:T(8,128)S(1)}, f32[512,128]{1,0:T(8,128)S(1)}, f32[512,128]{1,0:T(8...) custom-call(f32[1024,128]{1,0:T(8,128)S(1)} %get-tuple-element.31.fi, ...), custom_call_target="tpu_custom_call" | custom-call | flops 2621440 | bytes 2441216 | tf_op jit(solution)/shard_map/block/pallas_call | solution.py:468
  9.1 0.7 %collective-permute-start.1 = (f32[160,128]{1,0:T(8,128)S(1)}, f32[160,128]{1,0:T(8,128)S(1)}, u32[]{:S(2)}, u32[]{:S(2)}) collective-permute-start(f32[160,128]{1,0:T(8,128)S(1)} %get-tuple-element.47.rows_b.refs_6_), channel_id=1, source_target_pairs={{0,3},{1,2},{2,1},{3,0},{4,7},{5,6},{6,5},{7,4},{8,11},{9,10},{10,... | collective-permute-start | bytes 245768 | tf_op jit(solution)/shard_map/ppermute | solution.py:432
  9.9 0.1 later.1
  9.9 0.1 collective-permute-start.2
  10.0 1.0 %collective-permute-start = (f32[160,128]{1,0:T(8,128)S(1)}, f32[160,128]{1,0:T(8,128)S(1)}, u32[]{:S(2)}, u32[]{:S(2)}) collective-permute-start(f32[160,128]{1,0:T(8,128)S(1)} %get-tuple-element.48.refs_5_), channel_id=1, source_target_pairs={{0,1},{1,0},{2,3},{3,2},{4,5},{5,4},{6,7},{7,6},{8,9},{9,8},{10,11... | collective-permute-start | bytes 245768 | tf_op jit(solution)/shard_map/ppermute | solution.py:432
  11.0 0.8 %interior.1 = (f32[1024,128]{1,0:T(8,128)S(1)}, f32[16,128]{1,0:T(8,128)S(1)}, f32[64,128]{1,0:T(8,128)S(1)}) custom-call(f32[1024,128]{1,0:T(8,128)S(1)} %get-tuple-element.31.field.refs_0_, f32[1024,128]{1,0:T(8,128)S(1)} %get-tuple-element.37.image.refs_0_, f32[512,128]{1,0:T(8,128)S(1)} %get-tuple-element.38.coef_east.refs_2_, ...), custom_call_target="tpu_custom_call" | custom-call | flops 7864320000 | bytes 565248 | tf_op jit(solution)/shard_map/interior/pallas_call | solution.py:474
  11.8 0.0 collective-permute-done.3.refs_11_
  11.8 2.1 %collective-permute-done.2.refs_10_ = f32[32,128]{1,0:T(8,128)S(1)} collective-permute-done((f32[32,128]{1,0:T(8,128)S(1)}, f32[32,128]{1,0:T(8,128)S(1)}, u32[]{:S(2)}, u32[]{:S(2)}) %collective-permute-start.2) | collective-permute-done | bytes 16416 | tf_op jit(solution)/shard_map/ppermute | solution.py:432
  13.9 0.0 collective-permute-done.refs_7_
  13.9 0.0 collective-permute-done.1.refs_8_
  13.9 0.4 %sums.1 = (f32[1024,128]{1,0:T(8,128)S(1)}, f32[1024,128]{1,0:T(8,128)S(1)}, f32[56,128]{1,0:T(8,128)S(1)}, f32[128,128]{1,0:T(8,128)S(1)}) custom-call(f32[1024,128]{1,0:T(8,128)S(1)} %get-tuple-element.37.image.refs_0_, f32[1024,128]{1,0:T(8,128)S(1)} %get-tuple-element.43.refs_1_, ...), custom_call_target="tpu_custom_call", output_to_operand_aliasing={{0}: (0, {}), {1}: (1, {})} | custom-call | flops 131072 | bytes 1142784 | tf_op jit(solution)/shard_map/sums/pallas_call | solution.py:479
  14.3 9.5 %all_to_all.5 = f32[32,1,512]{2,1,0:T(1,128)S(1)} all-to-all(f32[32,1,512]{2,1,0:T(1,128)S(1)} %bitcast.10), channel_id=1, replica_groups=mesh['lon'=8,'lat'=4] {'lon','lat'}, dimensions={0} | all-to-all | bytes 131072 | tf_op jit(solution)/shard_map/all_to_all | solution.py:483
  23.9 1.4 %finish.1 = (f32[1024,128]{1,0:T(8,128)}, f32[1024,128]{1,0:T(8,128)}) custom-call(f32[1024,128]{1,0:T(8,128)S(1)} %get-tuple-element.31.field.refs_0_, f32[1024,128]{1,0:T(8,128)S(1)} %get-tuple-element.54.refs_1_, f32[1024,128]{1,0:T(8,128)S(1)} %get-tuple-element.55.refs_2_, f32[56,128]{1,0:T(8,128)S(1)} %get-tuple-element.56.refs_3_, f32[128,128]{1,0:T(8,128)S(1)} %bitcast.9), custom_call_target="tpu_custom_call" | custom-call | flops 2621440 | bytes 1048576 | tf_op jit(solution)/shard_map/finish/pallas_call | solution.py:485
Async XLA Ops:
  2.4 9.4 %collective-permute-start.3 = (f32[32,128]{1,0:T(8,128)S(1)}, f32[32,128]{1,0:T(8,128)S(1)}, u32[]{:S(2)}, u32[]{:S(2)}) collective-permute-start(f32[32,128]{1,0:T(8,128)S(1)} %get-tuple-element.50), channel_id=1, source_target_pairs={{0,28},{4,8},{8,4},{12,16},{16,12},{20,24},{24,20},{28,0},{1,29},{... | collective-permute-start | bytes 49160 | tf_op jit(solution)/shard_map/ppermute | solution.py:432
  9.1 4.8 %collective-permute-start.1 = (f32[160,128]{1,0:T(8,128)S(1)}, f32[160,128]{1,0:T(8,128)S(1)}, u32[]{:S(2)}, u32[]{:S(2)}) collective-permute-start(f32[160,128]{1,0:T(8,128)S(1)} %get-tuple-element.47.rows_b.refs_6_), channel_id=1, source_target_pairs={{0,3},{1,2},{2,1},{3,0},{4,7},{5,6},{6,5},{7,4},{8,11},{9,10},{10,... | collective-permute-start | bytes 245768 | tf_op jit(solution)/shard_map/ppermute | solution.py:432
  9.9 4.0 %collective-permute-start.2 = (f32[32,128]{1,0:T(8,128)S(1)}, f32[32,128]{1,0:T(8,128)S(1)}, u32[]{:S(2)}, u32[]{:S(2)}) collective-permute-start(f32[32,128]{1,0:T(8,128)S(1)} %get-tuple-element.49), channel_id=1, source_target_pairs={{0,4},{4,0},{8,12},{12,8},{16,20},{20,16},{24,28},{28,24},{1,5},{5... | collective-permute-start | bytes 49160 | tf_op jit(solution)/shard_map/ppermute | solution.py:432
  10.0 3.9 %collective-permute-start = (f32[160,128]{1,0:T(8,128)S(1)}, f32[160,128]{1,0:T(8,128)S(1)}, u32[]{:S(2)}, u32[]{:S(2)}) collective-permute-start(f32[160,128]{1,0:T(8,128)S(1)} %get-tuple-element.48.refs_5_), channel_id=1, source_target_pairs={{0,1},{1,0},{2,3},{3,2},{4,5},{5,4},{6,7},{7,6},{8,9},{9,8},{10,11... | collective-permute-start | bytes 245768 | tf_op jit(solution)/shard_map/ppermute | solution.py:432

commit v2 on v1

--- a/solution.py
+++ b/solution.py
@@ -369,7 +369,13 @@
     cross = jnp.sum(cross, axis=0, keepdims=True)
 
     lon, lat = lax.axis_index("lon"), lax.axis_index("lat")
-    share = lambda i, j, at: sums[pl.ds(SHARES * (i * along + j) + at, 1), :]
+    tile_row = iota((8, lanes), 0)
+
+    def share(i, j, at):
+        first = SHARES * (i * along + j)
+        tile = sums[pl.ds(pl.multiple_of(first // 8 * 8, 8), 8), :]
+        return jnp.sum(jnp.where(tile_row == lax.rem(first, 8) + at, tile, 0.0), axis=0, keepdims=True)
+
     faces = corrections[pl.ds(3 * rows, 8), :]
     east, west = lax.rem(lon + 1, across), lax.rem(lon + across - 1, across)
     south, north = jnp.maximum(lat - 1, 0), jnp.minimum(lat + 1, along - 1)
@@ -399,10 +405,11 @@
         whole = 1.0 / (bb + bw)
         step = bb * whole
         rest = bw * whole
-        beta = step * (ww * whole) - rest * rest
+        beta = jnp.maximum(step * (ww * whole) - rest * rest, 0.0)
         new = beta * bb
         tau = beta + rest
         step_next = new / (new + beta * new + tau * tau * bw - 2.0 * tau * step * ww + step * step * wy)
+        step_next = jnp.minimum(jnp.maximum(step_next, 0.0), 1.0)
         both = step * step_next
         s_b = step + step_next * tau
         r_b = rest - step_next * tau

time: 25.5 us -> 25.5 us (level)
  no operation moved by 1% of the time
where the time goes in v2:
time: 25.5 us; the launch traced here: 25.3 us
  blocking collectives  9.52 us (37%)
  starting transfers between devices  7.87 us (31%)
  Pallas kernels  5.15 us (20%)
  waiting for transfers between devices  2.12 us (8%)
  between operations  0.66 us (3%)
    all_to_all x1, blocking collectives, body(): lax.all_to_all(sums.reshape(devices, 1, -1), ('lon', 'lat'), 0, 0, tiled=...  9.52 us
    ppermute x4, starting transfers between devices, swapped(): lax.ppermute(x, axis, [(i, (i + 1 if forward[i] else i - 1) % devices) fo...  7.87 us
    ppermute x4, waiting for transfers between devices, swapped(): lax.ppermute(x, axis, [(i, (i + 1 if forward[i] else i - 1) % devices) fo...  2.12 us
    pallas_call x1, Pallas kernels, body(): call(columns_kernel, [tracers * n, (n, jnp.int32), (rows, jnp.int32)] + [...  1.76 us
    pallas_call x1, Pallas kernels, body(): call(with_devices(finish_kernel), [tracers * n] * 2, 20 * cells, space=ja...  1.44 us
    pallas_call x1, Pallas kernels, body(): call(interior_kernel, [tracers * n, rows, 8 * 4 * tracers], 60000 * cells...  0.75 us
    pallas_call x1, Pallas kernels, body(): call(block_kernel, [n] * 7 + [tracers * n, FIELDS * nz], 20 * cells, name...  0.69 us
  transfers between devices with their start and end apart: 4, of which 1 were waited for; matrix products, arithmetic and copies ran while one was open for 0% of the time, Pallas kernels for 6%

profile of v2, /device:TPU:0, one launch (start us, length us, event | category | flops | bytes accessed | tf_op | source)
XLA Modules:
  0.0 25.3 jit_solution(16348098627114023089)
XLA Ops:
  0.6 1.8 %columns.1 = (f32[1024,128]{1,0:T(8,128)S(1)}, s32[512,128]{1,0:T(8,128)S(1)}, s32[16,128]{1,0:T(8,128)S(1)}, bf16[512,128]{1,0:T(8,128)(2,1)S(1)}, bf16[512,128...) custom-call(f32[1024,128]{1,0:T(8,128)} %bitcast.11, ...), custom_call_target="tpu_custom_call" | custom-call | flops 2621440 | bytes 1646592 | tf_op jit(solution)/shard_map/columns/pallas_call | solution.py:465
  2.4 6.0 %collective-permute-start.3 = (f32[32,128]{1,0:T(8,128)S(1)}, f32[32,128]{1,0:T(8,128)S(1)}, u32[]{:S(2)}, u32[]{:S(2)}) collective-permute-start(f32[32,128]{1,0:T(8,128)S(1)} %get-tuple-element.50), channel_id=1, source_target_pairs={{0,28},{4,8},{8,4},{12,16},{16,12},{20,24},{24,20},{28,0},{1,29},{... | collective-permute-start | bytes 49160 | tf_op jit(solution)/shard_map/ppermute | solution.py:439
  8.4 0.7 %block.1 = (f32[512,128]{1,0:T(8,128)S(1)}, f32[512,128]{1,0:T(8,128)S(1)}, f32[512,128]{1,0:T(8,128)S(1)}, f32[512,128]{1,0:T(8,128)S(1)}, f32[512,128]{1,0:T(8...) custom-call(f32[1024,128]{1,0:T(8,128)S(1)} %get-tuple-element.31.fi, ...), custom_call_target="tpu_custom_call" | custom-call | flops 2621440 | bytes 2441216 | tf_op jit(solution)/shard_map/block/pallas_call | solution.py:475
  9.1 0.7 %collective-permute-start.1 = (f32[160,128]{1,0:T(8,128)S(1)}, f32[160,128]{1,0:T(8,128)S(1)}, u32[]{:S(2)}, u32[]{:S(2)}) collective-permute-start(f32[160,128]{1,0:T(8,128)S(1)} %get-tuple-element.47.rows_b.refs_6_), channel_id=1, source_target_pairs={{0,3},{1,2},{2,1},{3,0},{4,7},{5,6},{6,5},{7,4},{8,11},{9,10},{10,... | collective-permute-start | bytes 245768 | tf_op jit(solution)/shard_map/ppermute | solution.py:439
  9.9 0.1 later.1
  9.9 0.1 collective-permute-start.2
  10.0 1.0 %collective-permute-start = (f32[160,128]{1,0:T(8,128)S(1)}, f32[160,128]{1,0:T(8,128)S(1)}, u32[]{:S(2)}, u32[]{:S(2)}) collective-permute-start(f32[160,128]{1,0:T(8,128)S(1)} %get-tuple-element.48.refs_5_), channel_id=1, source_target_pairs={{0,1},{1,0},{2,3},{3,2},{4,5},{5,4},{6,7},{7,6},{8,9},{9,8},{10,11... | collective-permute-start | bytes 245768 | tf_op jit(solution)/shard_map/ppermute | solution.py:439
  11.0 0.8 %interior.1 = (f32[1024,128]{1,0:T(8,128)S(1)}, f32[16,128]{1,0:T(8,128)S(1)}, f32[64,128]{1,0:T(8,128)S(1)}) custom-call(f32[1024,128]{1,0:T(8,128)S(1)} %get-tuple-element.31.field.refs_0_, f32[1024,128]{1,0:T(8,128)S(1)} %get-tuple-element.37.image.refs_0_, f32[512,128]{1,0:T(8,128)S(1)} %get-tuple-element.38.coef_east.refs_2_, ...), custom_call_target="tpu_custom_call" | custom-call | flops 7864320000 | bytes 565248 | tf_op jit(solution)/shard_map/interior/pallas_call | solution.py:481
  11.8 0.0 collective-permute-done.3.refs_11_
  11.8 2.1 %collective-permute-done.2.refs_10_ = f32[32,128]{1,0:T(8,128)S(1)} collective-permute-done((f32[32,128]{1,0:T(8,128)S(1)}, f32[32,128]{1,0:T(8,128)S(1)}, u32[]{:S(2)}, u32[]{:S(2)}) %collective-permute-start.2) | collective-permute-done | bytes 16416 | tf_op jit(solution)/shard_map/ppermute | solution.py:439
  13.9 0.0 collective-permute-done.refs_7_
  13.9 0.0 collective-permute-done.1.refs_8_
  13.9 0.4 %sums.1 = (f32[1024,128]{1,0:T(8,128)S(1)}, f32[1024,128]{1,0:T(8,128)S(1)}, f32[56,128]{1,0:T(8,128)S(1)}, f32[128,128]{1,0:T(8,128)S(1)}) custom-call(f32[1024,128]{1,0:T(8,128)S(1)} %get-tuple-element.37.image.refs_0_, f32[1024,128]{1,0:T(8,128)S(1)} %get-tuple-element.43.refs_1_, ...), custom_call_target="tpu_custom_call", output_to_operand_aliasing={{0}: (0, {}), {1}: (1, {})} | custom-call | flops 131072 | bytes 1142784 | tf_op jit(solution)/shard_map/sums/pallas_call | solution.py:486
  14.3 9.5 %all_to_all.5 = f32[32,1,512]{2,1,0:T(1,128)S(1)} all-to-all(f32[32,1,512]{2,1,0:T(1,128)S(1)} %bitcast.10), channel_id=1, replica_groups=mesh['lon'=8,'lat'=4] {'lon','lat'}, dimensions={0} | all-to-all | bytes 131072 | tf_op jit(solution)/shard_map/all_to_all | solution.py:490
  23.9 1.4 %finish.1 = (f32[1024,128]{1,0:T(8,128)}, f32[1024,128]{1,0:T(8,128)}) custom-call(f32[1024,128]{1,0:T(8,128)S(1)} %get-tuple-element.31.field.refs_0_, f32[1024,128]{1,0:T(8,128)S(1)} %get-tuple-element.54.refs_1_, f32[1024,128]{1,0:T(8,128)S(1)} %get-tuple-element.55.refs_2_, f32[56,128]{1,0:T(8,128)S(1)} %get-tuple-element.56.refs_3_, f32[128,128]{1,0:T(8,128)S(1)} %bitcast.9), custom_call_target="tpu_custom_call" | custom-call | flops 2621440 | bytes 1048576 | tf_op jit(solution)/shard_map/finish/pallas_call | solution.py:492
Async XLA Ops:
  2.4 9.4 %collective-permute-start.3 = (f32[32,128]{1,0:T(8,128)S(1)}, f32[32,128]{1,0:T(8,128)S(1)}, u32[]{:S(2)}, u32[]{:S(2)}) collective-permute-start(f32[32,128]{1,0:T(8,128)S(1)} %get-tuple-element.50), channel_id=1, source_target_pairs={{0,28},{4,8},{8,4},{12,16},{16,12},{20,24},{24,20},{28,0},{1,29},{... | collective-permute-start | bytes 49160 | tf_op jit(solution)/shard_map/ppermute | solution.py:439
  9.1 4.8 %collective-permute-start.1 = (f32[160,128]{1,0:T(8,128)S(1)}, f32[160,128]{1,0:T(8,128)S(1)}, u32[]{:S(2)}, u32[]{:S(2)}) collective-permute-start(f32[160,128]{1,0:T(8,128)S(1)} %get-tuple-element.47.rows_b.refs_6_), channel_id=1, source_target_pairs={{0,3},{1,2},{2,1},{3,0},{4,7},{5,6},{6,5},{7,4},{8,11},{9,10},{10,... | collective-permute-start | bytes 245768 | tf_op jit(solution)/shard_map/ppermute | solution.py:439
  9.9 4.0 %collective-permute-start.2 = (f32[32,128]{1,0:T(8,128)S(1)}, f32[32,128]{1,0:T(8,128)S(1)}, u32[]{:S(2)}, u32[]{:S(2)}) collective-permute-start(f32[32,128]{1,0:T(8,128)S(1)} %get-tuple-element.49), channel_id=1, source_target_pairs={{0,4},{4,0},{8,12},{12,8},{16,20},{20,16},{24,28},{28,24},{1,5},{5... | collective-permute-start | bytes 49160 | tf_op jit(solution)/shard_map/ppermute | solution.py:439
  10.0 3.9 %collective-permute-start = (f32[160,128]{1,0:T(8,128)S(1)}, f32[160,128]{1,0:T(8,128)S(1)}, u32[]{:S(2)}, u32[]{:S(2)}) collective-permute-start(f32[160,128]{1,0:T(8,128)S(1)} %get-tuple-element.48.refs_5_), channel_id=1, source_target_pairs={{0,1},{1,0},{2,3},{3,2},{4,5},{5,4},{6,7},{7,6},{8,9},{9,8},{10,11... | collective-permute-start | bytes 245768 | tf_op jit(solution)/shard_map/ppermute | solution.py:439

commit v3 on v2

--- a/solution.py
+++ b/solution.py
@@ -361,8 +361,9 @@
     total, to_north, lon_south, mixed = [sums[pl.ds(i, devices, SHARES), :] for i in range(SHARES)]
     total = jnp.sum(total, axis=0, keepdims=True)
     even_lane = (iota((devices, lanes), 1) & 1) == 0
-    from_east = lambda x: pltpu.roll(pltpu.roll(x, devices - along, 0), lanes - 1, 1)
-    from_north = lambda x: pltpu.roll(x, devices - 1, 0)
+    last = lax.rem(iota((devices, lanes), 0), across) == across - 1
+    from_east = lambda x: pltpu.roll(jnp.where(last, pltpu.roll(x, across - 1, 0), pltpu.roll(x, devices - 1, 0)), lanes - 1, 1)
+    from_north = lambda x: pltpu.roll(x, devices - across, 0)
     beyond = from_east(lon_south)
     cross = jnp.where(even_lane, lon_south * beyond - mixed * from_north(beyond), 0.0)
     cross = cross + to_north * from_north(jnp.where(even_lane, -from_east(mixed), mixed))
@@ -372,7 +373,7 @@
     tile_row = iota((8, lanes), 0)
 
     def share(i, j, at):
-        first = SHARES * (i * along + j)
+        first = SHARES * (j * across + i)
         tile = sums[pl.ds(pl.multiple_of(first // 8 * 8, 8), 8), :]
         return jnp.sum(jnp.where(tile_row == lax.rem(first, 8) + at, tile, 0.0), axis=0, keepdims=True)
 
@@ -397,7 +398,7 @@
     def number(i):
         return jnp.sum(jnp.where(one == i, total, 0.0), axis=1, keepdims=True)
 
-    copies = []
+    copies, factors = [], []
     for t in range(tracers):
         bb, bw, ww, wy = [number(4 * t + i) for i in range(4)]
         mine = lax.rem(one >> 1, tracers) == t
@@ -411,9 +412,8 @@
         step_next = new / (new + beta * new + tau * tau * bw - 2.0 * tau * step * ww + step * step * wy)
         step_next = jnp.minimum(jnp.maximum(step_next, 0.0), 1.0)
         both = step * step_next
-        s_b = step + step_next * tau
-        r_b = rest - step_next * tau
-        r_w = both - step - step_next * tau
+        factors.append((both, step + step_next * tau, rest - step_next * tau, both - step - step_next * tau))
+    for t, (both, s_b, r_b, r_w) in enumerate(factors):
         s_edge = -both * e
         r_edge = jnp.where(lax.rem(narrow >> 1, tracers) == t, r_w * e + both * change,
                            both * jnp.where((narrow & 1) == 0, pltpu.roll(beside, 1, 1), pltpu.roll(beside, lanes - 1, 1)))
@@ -487,7 +487,7 @@
         with_devices(sums_kernel), [tracers * n, tracers * n, 3 * rows + 8, SHARES * devices], cells,
         input_output_aliases={0: 0, 1: 1}, name="sums",
     )(image, twice, coef_east, coef_north, coef_down, rows_a, rows_b, got_rows_a, got_rows_b, own, got_a, got_b, packed, packed_twice, sums)
-    sums = lax.all_to_all(sums.reshape(devices, 1, -1), ("lon", "lat"), 0, 0, tiled=True).reshape(-1, lanes)
+    sums = lax.all_to_all(sums.reshape(devices, 1, -1), ("lat", "lon"), 0, 0, tiled=True).reshape(-1, lanes)
     copies = 2 * tracers * nz // CHUNK
     solution_field, residual = call(
         with_devices(finish_kernel), [tracers * n] * 2, 20 * cells, space=jax.ShapeDtypeStruct,

time: 25.5 us -> 25.4 us (level)
  no operation moved by 1% of the time
where the time goes in v3:
time: 25.4 us; the launch traced here: 25.1 us
  blocking collectives  9.38 us (37%)
  starting transfers between devices  7.87 us (31%)
  Pallas kernels  5.11 us (20%)
  waiting for transfers between devices  2.12 us (8%)
  between operations  0.66 us (3%)
    all_to_all x1, blocking collectives, body(): lax.all_to_all(sums.reshape(devices, 1, -1), ('lat', 'lon'), 0, 0, tiled=...  9.38 us
    ppermute x4, starting transfers between devices, swapped(): lax.ppermute(x, axis, [(i, (i + 1 if forward[i] else i - 1) % devices) fo...  7.87 us
    ppermute x4, waiting for transfers between devices, swapped(): lax.ppermute(x, axis, [(i, (i + 1 if forward[i] else i - 1) % devices) fo...  2.12 us
    pallas_call x1, Pallas kernels, body(): call(columns_kernel, [tracers * n, (n, jnp.int32), (rows, jnp.int32)] + [...  1.76 us
    pallas_call x1, Pallas kernels, body(): call(with_devices(finish_kernel), [tracers * n] * 2, 20 * cells, space=ja...  1.41 us
    pallas_call x1, Pallas kernels, body(): call(interior_kernel, [tracers * n, rows, 8 * 4 * tracers], 60000 * cells...  0.75 us
    pallas_call x1, Pallas kernels, body(): call(block_kernel, [n] * 7 + [tracers * n, FIELDS * nz], 20 * cells, name...  0.69 us
  transfers between devices with their start and end apart: 4, of which 1 were waited for; matrix products, arithmetic and copies ran while one was open for 0% of the time, Pallas kernels for 6%

profile of v3, /device:TPU:0, one launch (start us, length us, event | category | flops | bytes accessed | tf_op | source)
XLA Modules:
  0.0 25.1 jit_solution(3226309192836823675)
XLA Ops:
  0.6 1.8 %columns.1 = (f32[1024,128]{1,0:T(8,128)S(1)}, s32[512,128]{1,0:T(8,128)S(1)}, s32[16,128]{1,0:T(8,128)S(1)}, bf16[512,128]{1,0:T(8,128)(2,1)S(1)}, bf16[512,128...) custom-call(f32[1024,128]{1,0:T(8,128)} %bitcast.11, ...), custom_call_target="tpu_custom_call" | custom-call | flops 2621440 | bytes 1646592 | tf_op jit(solution)/shard_map/columns/pallas_call | solution.py:465
  2.4 6.0 %collective-permute-start.3 = (f32[32,128]{1,0:T(8,128)S(1)}, f32[32,128]{1,0:T(8,128)S(1)}, u32[]{:S(2)}, u32[]{:S(2)}) collective-permute-start(f32[32,128]{1,0:T(8,128)S(1)} %get-tuple-element.50), channel_id=1, source_target_pairs={{0,28},{4,8},{8,4},{12,16},{16,12},{20,24},{24,20},{28,0},{1,29},{... | collective-permute-start | bytes 49160 | tf_op jit(solution)/shard_map/ppermute | solution.py:439
  8.4 0.7 %block.1 = (f32[512,128]{1,0:T(8,128)S(1)}, f32[512,128]{1,0:T(8,128)S(1)}, f32[512,128]{1,0:T(8,128)S(1)}, f32[512,128]{1,0:T(8,128)S(1)}, f32[512,128]{1,0:T(8...) custom-call(f32[1024,128]{1,0:T(8,128)S(1)} %get-tuple-element.31.fi, ...), custom_call_target="tpu_custom_call" | custom-call | flops 2621440 | bytes 2441216 | tf_op jit(solution)/shard_map/block/pallas_call | solution.py:475
  9.1 0.7 %collective-permute-start.1 = (f32[160,128]{1,0:T(8,128)S(1)}, f32[160,128]{1,0:T(8,128)S(1)}, u32[]{:S(2)}, u32[]{:S(2)}) collective-permute-start(f32[160,128]{1,0:T(8,128)S(1)} %get-tuple-element.47.rows_b.refs_6_), channel_id=1, source_target_pairs={{0,3},{1,2},{2,1},{3,0},{4,7},{5,6},{6,5},{7,4},{8,11},{9,10},{10,... | collective-permute-start | bytes 245768 | tf_op jit(solution)/shard_map/ppermute | solution.py:439
  9.9 0.1 later.1
  9.9 0.1 collective-permute-start.2
  10.0 1.0 %collective-permute-start = (f32[160,128]{1,0:T(8,128)S(1)}, f32[160,128]{1,0:T(8,128)S(1)}, u32[]{:S(2)}, u32[]{:S(2)}) collective-permute-start(f32[160,128]{1,0:T(8,128)S(1)} %get-tuple-element.48.refs_5_), channel_id=1, source_target_pairs={{0,1},{1,0},{2,3},{3,2},{4,5},{5,4},{6,7},{7,6},{8,9},{9,8},{10,11... | collective-permute-start | bytes 245768 | tf_op jit(solution)/shard_map/ppermute | solution.py:439
  11.0 0.8 %interior.1 = (f32[1024,128]{1,0:T(8,128)S(1)}, f32[16,128]{1,0:T(8,128)S(1)}, f32[64,128]{1,0:T(8,128)S(1)}) custom-call(f32[1024,128]{1,0:T(8,128)S(1)} %get-tuple-element.31.field.refs_0_, f32[1024,128]{1,0:T(8,128)S(1)} %get-tuple-element.37.image.refs_0_, f32[512,128]{1,0:T(8,128)S(1)} %get-tuple-element.38.coef_east.refs_2_, ...), custom_call_target="tpu_custom_call" | custom-call | flops 7864320000 | bytes 565248 | tf_op jit(solution)/shard_map/interior/pallas_call | solution.py:481
  11.8 0.0 collective-permute-done.3.refs_11_
  11.8 2.1 %collective-permute-done.2.refs_10_ = f32[32,128]{1,0:T(8,128)S(1)} collective-permute-done((f32[32,128]{1,0:T(8,128)S(1)}, f32[32,128]{1,0:T(8,128)S(1)}, u32[]{:S(2)}, u32[]{:S(2)}) %collective-permute-start.2) | collective-permute-done | bytes 16416 | tf_op jit(solution)/shard_map/ppermute | solution.py:439
  13.9 0.0 collective-permute-done.refs_7_
  13.9 0.0 collective-permute-done.1.refs_8_
  13.9 0.4 %sums.1 = (f32[1024,128]{1,0:T(8,128)S(1)}, f32[1024,128]{1,0:T(8,128)S(1)}, f32[56,128]{1,0:T(8,128)S(1)}, f32[128,128]{1,0:T(8,128)S(1)}) custom-call(f32[1024,128]{1,0:T(8,128)S(1)} %get-tuple-element.37.image.refs_0_, f32[1024,128]{1,0:T(8,128)S(1)} %get-tuple-element.43.refs_1_, ...), custom_call_target="tpu_custom_call", output_to_operand_aliasing={{0}: (0, {}), {1}: (1, {})} | custom-call | flops 131072 | bytes 1142784 | tf_op jit(solution)/shard_map/sums/pallas_call | solution.py:486
  14.3 9.4 %all_to_all.5 = f32[32,1,512]{2,1,0:T(1,128)S(1)} all-to-all(f32[32,1,512]{2,1,0:T(1,128)S(1)} %bitcast.10), channel_id=1, replica_groups=mesh['lon'=8,'lat'=4] {'lat','lon'}, dimensions={0} | all-to-all | bytes 131072 | tf_op jit(solution)/shard_map/all_to_all | solution.py:490
  23.7 1.4 %finish.1 = (f32[1024,128]{1,0:T(8,128)}, f32[1024,128]{1,0:T(8,128)}) custom-call(f32[1024,128]{1,0:T(8,128)S(1)} %get-tuple-element.31.field.refs_0_, f32[1024,128]{1,0:T(8,128)S(1)} %get-tuple-element.54.refs_1_, f32[1024,128]{1,0:T(8,128)S(1)} %get-tuple-element.55.refs_2_, f32[56,128]{1,0:T(8,128)S(1)} %get-tuple-element.56.refs_3_, f32[128,128]{1,0:T(8,128)S(1)} %bitcast.9), custom_call_target="tpu_custom_call" | custom-call | flops 2621440 | bytes 1048576 | tf_op jit(solution)/shard_map/finish/pallas_call | solution.py:492
Async XLA Ops:
  2.4 9.4 %collective-permute-start.3 = (f32[32,128]{1,0:T(8,128)S(1)}, f32[32,128]{1,0:T(8,128)S(1)}, u32[]{:S(2)}, u32[]{:S(2)}) collective-permute-start(f32[32,128]{1,0:T(8,128)S(1)} %get-tuple-element.50), channel_id=1, source_target_pairs={{0,28},{4,8},{8,4},{12,16},{16,12},{20,24},{24,20},{28,0},{1,29},{... | collective-permute-start | bytes 49160 | tf_op jit(solution)/shard_map/ppermute | solution.py:439
  9.1 4.8 %collective-permute-start.1 = (f32[160,128]{1,0:T(8,128)S(1)}, f32[160,128]{1,0:T(8,128)S(1)}, u32[]{:S(2)}, u32[]{:S(2)}) collective-permute-start(f32[160,128]{1,0:T(8,128)S(1)} %get-tuple-element.47.rows_b.refs_6_), channel_id=1, source_target_pairs={{0,3},{1,2},{2,1},{3,0},{4,7},{5,6},{6,5},{7,4},{8,11},{9,10},{10,... | collective-permute-start | bytes 245768 | tf_op jit(solution)/shard_map/ppermute | solution.py:439
  9.9 4.0 %collective-permute-start.2 = (f32[32,128]{1,0:T(8,128)S(1)}, f32[32,128]{1,0:T(8,128)S(1)}, u32[]{:S(2)}, u32[]{:S(2)}) collective-permute-start(f32[32,128]{1,0:T(8,128)S(1)} %get-tuple-element.49), channel_id=1, source_target_pairs={{0,4},{4,0},{8,12},{12,8},{16,20},{20,16},{24,28},{28,24},{1,5},{5... | collective-permute-start | bytes 49160 | tf_op jit(solution)/shard_map/ppermute | solution.py:439
  10.0 3.9 %collective-permute-start = (f32[160,128]{1,0:T(8,128)S(1)}, f32[160,128]{1,0:T(8,128)S(1)}, u32[]{:S(2)}, u32[]{:S(2)}) collective-permute-start(f32[160,128]{1,0:T(8,128)S(1)} %get-tuple-element.48.refs_5_), channel_id=1, source_target_pairs={{0,1},{1,0},{2,3},{3,2},{4,5},{5,4},{6,7},{7,6},{8,9},{9,8},{10,11... | collective-permute-start | bytes 245768 | tf_op jit(solution)/shard_map/ppermute | solution.py:439

commit v4 on v3

--- a/solution.py
+++ b/solution.py
@@ -259,7 +259,9 @@
         first, next_row, between = ((0, 1, 0), (rows - 1, rows - 2, rows - 2))[side]
         c_east, c_down = coef_east[pl.ds(first, nz, rows), :], coef_down[pl.ds(first, nz, rows), :]
         c_inner = coef_north[pl.ds(between, nz, rows), :]
-        packed_coef, packed_ring, packed_e, packed_inside = [nothing] * 4
+        packed_ring, packed_e, packed_inside = [nothing] * 3
+        packed_coef = spread(c, 0, tracers, pair, level)
+        packed_coef = sum((pltpu.roll(packed_coef, 2 * t, 1) for t in range(1, tracers)), packed_coef)
         for t in range(tracers):
             b, w = own_row(tracers + t), own_row(t)
             f = c * (got_row(tracers + t) - b)
@@ -278,7 +280,6 @@
             stores.append((twice, at_next, twice_in[at_next, :] - c_inner * e))
             for i, value in enumerate((b * e, (w + changed) * e, (2.0 * y + inside) * e - changed * through)):
                 dots[t][i] = dots[t][i] + folded(value)
-            packed_coef = packed_coef + spread(c, t, tracers, pair, level)
             packed_ring = packed_ring + spread(ring, t, tracers, pair, level)
             packed_e = packed_e + spread(e, t, tracers, pair, level)
             packed_inside = packed_inside + spread(inside, t, tracers, pair, level)

time: 25.4 us -> 25.3 us (level)
  no operation moved by 1% of the time
where the time goes in v4:
time: 25.3 us; the launch traced here: 25.1 us
  blocking collectives  9.39 us (37%)
  starting transfers between devices  7.87 us (31%)
  Pallas kernels  5.1 us (20%)
  waiting for transfers between devices  2.12 us (8%)
  between operations  0.66 us (3%)
    all_to_all x1, blocking collectives, body(): lax.all_to_all(sums.reshape(devices, 1, -1), ('lat', 'lon'), 0, 0, tiled=...  9.39 us
    ppermute x4, starting transfers between devices, swapped(): lax.ppermute(x, axis, [(i, (i + 1 if forward[i] else i - 1) % devices) fo...  7.87 us
    ppermute x4, waiting for transfers between devices, swapped(): lax.ppermute(x, axis, [(i, (i + 1 if forward[i] else i - 1) % devices) fo...  2.12 us
    pallas_call x1, Pallas kernels, body(): call(columns_kernel, [tracers * n, (n, jnp.int32), (rows, jnp.int32)] + [...  1.76 us
    pallas_call x1, Pallas kernels, body(): call(with_devices(finish_kernel), [tracers * n] * 2, 20 * cells, space=ja...  1.41 us
    pallas_call x1, Pallas kernels, body(): call(interior_kernel, [tracers * n, rows, 8 * 4 * tracers], 60000 * cells...  0.75 us
    pallas_call x1, Pallas kernels, body(): call(block_kernel, [n] * 7 + [tracers * n, FIELDS * nz], 20 * cells, name...  0.69 us
  transfers between devices with their start and end apart: 4, of which 1 were waited for; matrix products, arithmetic and copies ran while one was open for 0% of the time, Pallas kernels for 6%

profile of v4, /device:TPU:0, one launch (start us, length us, event | category | flops | bytes accessed | tf_op | source)
XLA Modules:
  0.0 25.1 jit_solution(38070070854075995)
XLA Ops:
  0.6 1.8 %columns.1 = (f32[1024,128]{1,0:T(8,128)S(1)}, s32[512,128]{1,0:T(8,128)S(1)}, s32[16,128]{1,0:T(8,128)S(1)}, bf16[512,128]{1,0:T(8,128)(2,1)S(1)}, bf16[512,128...) custom-call(f32[1024,128]{1,0:T(8,128)} %bitcast.11, ...), custom_call_target="tpu_custom_call" | custom-call | flops 2621440 | bytes 1646592 | tf_op jit(solution)/shard_map/columns/pallas_call | solution.py:466
  2.4 6.0 %collective-permute-start.3 = (f32[32,128]{1,0:T(8,128)S(1)}, f32[32,128]{1,0:T(8,128)S(1)}, u32[]{:S(2)}, u32[]{:S(2)}) collective-permute-start(f32[32,128]{1,0:T(8,128)S(1)} %get-tuple-element.50), channel_id=1, source_target_pairs={{0,28},{4,8},{8,4},{12,16},{16,12},{20,24},{24,20},{28,0},{1,29},{... | collective-permute-start | bytes 49160 | tf_op jit(solution)/shard_map/ppermute | solution.py:440
  8.4 0.7 %block.1 = (f32[512,128]{1,0:T(8,128)S(1)}, f32[512,128]{1,0:T(8,128)S(1)}, f32[512,128]{1,0:T(8,128)S(1)}, f32[512,128]{1,0:T(8,128)S(1)}, f32[512,128]{1,0:T(8...) custom-call(f32[1024,128]{1,0:T(8,128)S(1)} %get-tuple-element.31.fi, ...), custom_call_target="tpu_custom_call" | custom-call | flops 2621440 | bytes 2441216 | tf_op jit(solution)/shard_map/block/pallas_call | solution.py:476
  9.1 0.7 %collective-permute-start.1 = (f32[160,128]{1,0:T(8,128)S(1)}, f32[160,128]{1,0:T(8,128)S(1)}, u32[]{:S(2)}, u32[]{:S(2)}) collective-permute-start(f32[160,128]{1,0:T(8,128)S(1)} %get-tuple-element.47.rows_b.refs_6_), channel_id=1, source_target_pairs={{0,3},{1,2},{2,1},{3,0},{4,7},{5,6},{6,5},{7,4},{8,11},{9,10},{10,... | collective-permute-start | bytes 245768 | tf_op jit(solution)/shard_map/ppermute | solution.py:440
  9.9 0.1 later.1
  9.9 0.1 collective-permute-start.2
  10.0 1.0 %collective-permute-start = (f32[160,128]{1,0:T(8,128)S(1)}, f32[160,128]{1,0:T(8,128)S(1)}, u32[]{:S(2)}, u32[]{:S(2)}) collective-permute-start(f32[160,128]{1,0:T(8,128)S(1)} %get-tuple-element.48.refs_5_), channel_id=1, source_target_pairs={{0,1},{1,0},{2,3},{3,2},{4,5},{5,4},{6,7},{7,6},{8,9},{9,8},{10,11... | collective-permute-start | bytes 245768 | tf_op jit(solution)/shard_map/ppermute | solution.py:440
  11.0 0.8 %interior.1 = (f32[1024,128]{1,0:T(8,128)S(1)}, f32[16,128]{1,0:T(8,128)S(1)}, f32[64,128]{1,0:T(8,128)S(1)}) custom-call(f32[1024,128]{1,0:T(8,128)S(1)} %get-tuple-element.31.field.refs_0_, f32[1024,128]{1,0:T(8,128)S(1)} %get-tuple-element.37.image.refs_0_, f32[512,128]{1,0:T(8,128)S(1)} %get-tuple-element.38.coef_east.refs_2_, ...), custom_call_target="tpu_custom_call" | custom-call | flops 7864320000 | bytes 565248 | tf_op jit(solution)/shard_map/interior/pallas_call | solution.py:482
  11.8 0.0 collective-permute-done.3.refs_11_
  11.8 2.1 %collective-permute-done.2.refs_10_ = f32[32,128]{1,0:T(8,128)S(1)} collective-permute-done((f32[32,128]{1,0:T(8,128)S(1)}, f32[32,128]{1,0:T(8,128)S(1)}, u32[]{:S(2)}, u32[]{:S(2)}) %collective-permute-start.2) | collective-permute-done | bytes 16416 | tf_op jit(solution)/shard_map/ppermute | solution.py:440
  13.9 0.0 collective-permute-done.refs_7_
  13.9 0.0 collective-permute-done.1.refs_8_
  13.9 0.4 %sums.1 = (f32[1024,128]{1,0:T(8,128)S(1)}, f32[1024,128]{1,0:T(8,128)S(1)}, f32[56,128]{1,0:T(8,128)S(1)}, f32[128,128]{1,0:T(8,128)S(1)}) custom-call(f32[1024,128]{1,0:T(8,128)S(1)} %get-tuple-element.37.image.refs_0_, f32[1024,128]{1,0:T(8,128)S(1)} %get-tuple-element.43.refs_1_, ...), custom_call_target="tpu_custom_call", output_to_operand_aliasing={{0}: (0, {}), {1}: (1, {})} | custom-call | flops 131072 | bytes 1142784 | tf_op jit(solution)/shard_map/sums/pallas_call | solution.py:487
  14.3 9.4 %all_to_all.5 = f32[32,1,512]{2,1,0:T(1,128)S(1)} all-to-all(f32[32,1,512]{2,1,0:T(1,128)S(1)} %bitcast.10), channel_id=1, replica_groups=mesh['lon'=8,'lat'=4] {'lat','lon'}, dimensions={0} | all-to-all | bytes 131072 | tf_op jit(solution)/shard_map/all_to_all | solution.py:491
  23.7 1.4 %finish.1 = (f32[1024,128]{1,0:T(8,128)}, f32[1024,128]{1,0:T(8,128)}) custom-call(f32[1024,128]{1,0:T(8,128)S(1)} %get-tuple-element.31.field.refs_0_, f32[1024,128]{1,0:T(8,128)S(1)} %get-tuple-element.54.refs_1_, f32[1024,128]{1,0:T(8,128)S(1)} %get-tuple-element.55.refs_2_, f32[56,128]{1,0:T(8,128)S(1)} %get-tuple-element.56.refs_3_, f32[128,128]{1,0:T(8,128)S(1)} %bitcast.9), custom_call_target="tpu_custom_call" | custom-call | flops 2621440 | bytes 1048576 | tf_op jit(solution)/shard_map/finish/pallas_call | solution.py:493
Async XLA Ops:
  2.4 9.4 %collective-permute-start.3 = (f32[32,128]{1,0:T(8,128)S(1)}, f32[32,128]{1,0:T(8,128)S(1)}, u32[]{:S(2)}, u32[]{:S(2)}) collective-permute-start(f32[32,128]{1,0:T(8,128)S(1)} %get-tuple-element.50), channel_id=1, source_target_pairs={{0,28},{4,8},{8,4},{12,16},{16,12},{20,24},{24,20},{28,0},{1,29},{... | collective-permute-start | bytes 49160 | tf_op jit(solution)/shard_map/ppermute | solution.py:440
  9.1 4.8 %collective-permute-start.1 = (f32[160,128]{1,0:T(8,128)S(1)}, f32[160,128]{1,0:T(8,128)S(1)}, u32[]{:S(2)}, u32[]{:S(2)}) collective-permute-start(f32[160,128]{1,0:T(8,128)S(1)} %get-tuple-element.47.rows_b.refs_6_), channel_id=1, source_target_pairs={{0,3},{1,2},{2,1},{3,0},{4,7},{5,6},{6,5},{7,4},{8,11},{9,10},{10,... | collective-permute-start | bytes 245768 | tf_op jit(solution)/shard_map/ppermute | solution.py:440
  9.9 4.0 %collective-permute-start.2 = (f32[32,128]{1,0:T(8,128)S(1)}, f32[32,128]{1,0:T(8,128)S(1)}, u32[]{:S(2)}, u32[]{:S(2)}) collective-permute-start(f32[32,128]{1,0:T(8,128)S(1)} %get-tuple-element.49), channel_id=1, source_target_pairs={{0,4},{4,0},{8,12},{12,8},{16,20},{20,16},{24,28},{28,24},{1,5},{5... | collective-permute-start | bytes 49160 | tf_op jit(solution)/shard_map/ppermute | solution.py:440
  10.0 3.9 %collective-permute-start = (f32[160,128]{1,0:T(8,128)S(1)}, f32[160,128]{1,0:T(8,128)S(1)}, u32[]{:S(2)}, u32[]{:S(2)}) collective-permute-start(f32[160,128]{1,0:T(8,128)S(1)} %get-tuple-element.48.refs_5_), channel_id=1, source_target_pairs={{0,1},{1,0},{2,3},{3,2},{4,5},{5,4},{6,7},{7,6},{8,9},{9,8},{10,11... | collective-permute-start | bytes 245768 | tf_op jit(solution)/shard_map/ppermute | solution.py:440

commit v5 on v3

--- a/solution.py
+++ b/solution.py
@@ -288,8 +288,6 @@
         lat_coef.append(packed_coef)
         lat_ring.append(packed_ring)
         lat_change.append(-packed_e)
-    for ref, at, value in stores:
-        ref[at, :] = value
 
     even = is_even("lon")
     even_lane = (iota((rows, lanes), 1) & 1) == 0
@@ -350,6 +348,8 @@
               jnp.where(even_row, lon_shares[1], f[south : south + 1])]
     for i, share in enumerate(shares):
         result[pl.ds(i, devices, SHARES), :] = jnp.broadcast_to(share, (devices, lanes))
+    for ref, at, value in stores:
+        ref[at, :] = value
 
 
 def finish_kernel(tracers, nz, rows, devices, field, image, twice, corrections, sums, solution_out, residual_out,

time: 25.4 us -> 25.4 us (level)
  no operation moved by 1% of the time
where the time goes in v5:
time: 25.4 us; the launch traced here: 25.1 us
  blocking collectives  9.38 us (37%)
  starting transfers between devices  7.87 us (31%)
  Pallas kernels  5.11 us (20%)
  waiting for transfers between devices  2.12 us (8%)
  between operations  0.66 us (3%)
    all_to_all x1, blocking collectives, body(): lax.all_to_all(sums.reshape(devices, 1, -1), ('lat', 'lon'), 0, 0, tiled=...  9.38 us
    ppermute x4, starting transfers between devices, swapped(): lax.ppermute(x, axis, [(i, (i + 1 if forward[i] else i - 1) % devices) fo...  7.87 us
    ppermute x4, waiting for transfers between devices, swapped(): lax.ppermute(x, axis, [(i, (i + 1 if forward[i] else i - 1) % devices) fo...  2.12 us
    pallas_call x1, Pallas kernels, body(): call(columns_kernel, [tracers * n, (n, jnp.int32), (rows, jnp.int32)] + [...  1.76 us
    pallas_call x1, Pallas kernels, body(): call(with_devices(finish_kernel), [tracers * n] * 2, 20 * cells, space=ja...  1.41 us
    pallas_call x1, Pallas kernels, body(): call(interior_kernel, [tracers * n, rows, 8 * 4 * tracers], 60000 * cells...  0.75 us
    pallas_call x1, Pallas kernels, body(): call(block_kernel, [n] * 7 + [tracers * n, FIELDS * nz], 20 * cells, name...  0.69 us
  transfers between devices with their start and end apart: 4, of which 1 were waited for; matrix products, arithmetic and copies ran while one was open for 0% of the time, Pallas kernels for 6%

profile of v5, /device:TPU:0, one launch (start us, length us, event | category | flops | bytes accessed | tf_op | source)
XLA Modules:
  0.0 25.1 jit_solution(3226309192836823675)
XLA Ops:
  0.6 1.8 %columns.1 = (f32[1024,128]{1,0:T(8,128)S(1)}, s32[512,128]{1,0:T(8,128)S(1)}, s32[16,128]{1,0:T(8,128)S(1)}, bf16[512,128]{1,0:T(8,128)(2,1)S(1)}, bf16[512,128...) custom-call(f32[1024,128]{1,0:T(8,128)} %bitcast.11, ...), custom_call_target="tpu_custom_call" | custom-call | flops 2621440 | bytes 1646592 | tf_op jit(solution)/shard_map/columns/pallas_call | solution.py:465
  2.4 6.0 %collective-permute-start.3 = (f32[32,128]{1,0:T(8,128)S(1)}, f32[32,128]{1,0:T(8,128)S(1)}, u32[]{:S(2)}, u32[]{:S(2)}) collective-permute-start(f32[32,128]{1,0:T(8,128)S(1)} %get-tuple-element.50), channel_id=1, source_target_pairs={{0,28},{4,8},{8,4},{12,16},{16,12},{20,24},{24,20},{28,0},{1,29},{... | collective-permute-start | bytes 49160 | tf_op jit(solution)/shard_map/ppermute | solution.py:439
  8.4 0.7 %block.1 = (f32[512,128]{1,0:T(8,128)S(1)}, f32[512,128]{1,0:T(8,128)S(1)}, f32[512,128]{1,0:T(8,128)S(1)}, f32[512,128]{1,0:T(8,128)S(1)}, f32[512,128]{1,0:T(8...) custom-call(f32[1024,128]{1,0:T(8,128)S(1)} %get-tuple-element.31.fi, ...), custom_call_target="tpu_custom_call" | custom-call | flops 2621440 | bytes 2441216 | tf_op jit(solution)/shard_map/block/pallas_call | solution.py:475
  9.1 0.7 %collective-permute-start.1 = (f32[160,128]{1,0:T(8,128)S(1)}, f32[160,128]{1,0:T(8,128)S(1)}, u32[]{:S(2)}, u32[]{:S(2)}) collective-permute-start(f32[160,128]{1,0:T(8,128)S(1)} %get-tuple-element.47.rows_b.refs_6_), channel_id=1, source_target_pairs={{0,3},{1,2},{2,1},{3,0},{4,7},{5,6},{6,5},{7,4},{8,11},{9,10},{10,... | collective-permute-start | bytes 245768 | tf_op jit(solution)/shard_map/ppermute | solution.py:439
  9.9 0.1 later.1
  9.9 0.1 collective-permute-start.2
  10.0 1.0 %collective-permute-start = (f32[160,128]{1,0:T(8,128)S(1)}, f32[160,128]{1,0:T(8,128)S(1)}, u32[]{:S(2)}, u32[]{:S(2)}) collective-permute-start(f32[160,128]{1,0:T(8,128)S(1)} %get-tuple-element.48.refs_5_), channel_id=1, source_target_pairs={{0,1},{1,0},{2,3},{3,2},{4,5},{5,4},{6,7},{7,6},{8,9},{9,8},{10,11... | collective-permute-start | bytes 245768 | tf_op jit(solution)/shard_map/ppermute | solution.py:439
  11.0 0.8 %interior.1 = (f32[1024,128]{1,0:T(8,128)S(1)}, f32[16,128]{1,0:T(8,128)S(1)}, f32[64,128]{1,0:T(8,128)S(1)}) custom-call(f32[1024,128]{1,0:T(8,128)S(1)} %get-tuple-element.31.field.refs_0_, f32[1024,128]{1,0:T(8,128)S(1)} %get-tuple-element.37.image.refs_0_, f32[512,128]{1,0:T(8,128)S(1)} %get-tuple-element.38.coef_east.refs_2_, ...), custom_call_target="tpu_custom_call" | custom-call | flops 7864320000 | bytes 565248 | tf_op jit(solution)/shard_map/interior/pallas_call | solution.py:481
  11.8 0.0 collective-permute-done.3.refs_11_
  11.8 2.1 %collective-permute-done.2.refs_10_ = f32[32,128]{1,0:T(8,128)S(1)} collective-permute-done((f32[32,128]{1,0:T(8,128)S(1)}, f32[32,128]{1,0:T(8,128)S(1)}, u32[]{:S(2)}, u32[]{:S(2)}) %collective-permute-start.2) | collective-permute-done | bytes 16416 | tf_op jit(solution)/shard_map/ppermute | solution.py:439
  13.9 0.0 collective-permute-done.refs_7_
  13.9 0.0 collective-permute-done.1.refs_8_
  13.9 0.4 %sums.1 = (f32[1024,128]{1,0:T(8,128)S(1)}, f32[1024,128]{1,0:T(8,128)S(1)}, f32[56,128]{1,0:T(8,128)S(1)}, f32[128,128]{1,0:T(8,128)S(1)}) custom-call(f32[1024,128]{1,0:T(8,128)S(1)} %get-tuple-element.37.image.refs_0_, f32[1024,128]{1,0:T(8,128)S(1)} %get-tuple-element.43.refs_1_, ...), custom_call_target="tpu_custom_call", output_to_operand_aliasing={{0}: (0, {}), {1}: (1, {})} | custom-call | flops 131072 | bytes 1142784 | tf_op jit(solution)/shard_map/sums/pallas_call | solution.py:486
  14.3 9.4 %all_to_all.5 = f32[32,1,512]{2,1,0:T(1,128)S(1)} all-to-all(f32[32,1,512]{2,1,0:T(1,128)S(1)} %bitcast.10), channel_id=1, replica_groups=mesh['lon'=8,'lat'=4] {'lat','lon'}, dimensions={0} | all-to-all | bytes 131072 | tf_op jit(solution)/shard_map/all_to_all | solution.py:490
  23.7 1.4 %finish.1 = (f32[1024,128]{1,0:T(8,128)}, f32[1024,128]{1,0:T(8,128)}) custom-call(f32[1024,128]{1,0:T(8,128)S(1)} %get-tuple-element.31.field.refs_0_, f32[1024,128]{1,0:T(8,128)S(1)} %get-tuple-element.54.refs_1_, f32[1024,128]{1,0:T(8,128)S(1)} %get-tuple-element.55.refs_2_, f32[56,128]{1,0:T(8,128)S(1)} %get-tuple-element.56.refs_3_, f32[128,128]{1,0:T(8,128)S(1)} %bitcast.9), custom_call_target="tpu_custom_call" | custom-call | flops 2621440 | bytes 1048576 | tf_op jit(solution)/shard_map/finish/pallas_call | solution.py:492
Async XLA Ops:
  2.4 9.4 %collective-permute-start.3 = (f32[32,128]{1,0:T(8,128)S(1)}, f32[32,128]{1,0:T(8,128)S(1)}, u32[]{:S(2)}, u32[]{:S(2)}) collective-permute-start(f32[32,128]{1,0:T(8,128)S(1)} %get-tuple-element.50), channel_id=1, source_target_pairs={{0,28},{4,8},{8,4},{12,16},{16,12},{20,24},{24,20},{28,0},{1,29},{... | collective-permute-start | bytes 49160 | tf_op jit(solution)/shard_map/ppermute | solution.py:439
  9.1 4.8 %collective-permute-start.1 = (f32[160,128]{1,0:T(8,128)S(1)}, f32[160,128]{1,0:T(8,128)S(1)}, u32[]{:S(2)}, u32[]{:S(2)}) collective-permute-start(f32[160,128]{1,0:T(8,128)S(1)} %get-tuple-element.47.rows_b.refs_6_), channel_id=1, source_target_pairs={{0,3},{1,2},{2,1},{3,0},{4,7},{5,6},{6,5},{7,4},{8,11},{9,10},{10,... | collective-permute-start | bytes 245768 | tf_op jit(solution)/shard_map/ppermute | solution.py:439
  9.9 4.0 %collective-permute-start.2 = (f32[32,128]{1,0:T(8,128)S(1)}, f32[32,128]{1,0:T(8,128)S(1)}, u32[]{:S(2)}, u32[]{:S(2)}) collective-permute-start(f32[32,128]{1,0:T(8,128)S(1)} %get-tuple-element.49), channel_id=1, source_target_pairs={{0,4},{4,0},{8,12},{12,8},{16,20},{20,16},{24,28},{28,24},{1,5},{5... | collective-permute-start | bytes 49160 | tf_op jit(solution)/shard_map/ppermute | solution.py:439
  10.0 3.9 %collective-permute-start = (f32[160,128]{1,0:T(8,128)S(1)}, f32[160,128]{1,0:T(8,128)S(1)}, u32[]{:S(2)}, u32[]{:S(2)}) collective-permute-start(f32[160,128]{1,0:T(8,128)S(1)} %get-tuple-element.48.refs_5_), channel_id=1, source_target_pairs={{0,1},{1,0},{2,3},{3,2},{4,5},{5,4},{6,7},{7,6},{8,9},{9,8},{10,11... | collective-permute-start | bytes 245768 | tf_op jit(solution)/shard_map/ppermute | solution.py:439
